TPU v7x, 32 devices: a whole 2x2x4 slice. The times are simulated.
32 devices in a mesh: groups: 2 (over x), docs: 16 (over z, y, core).
Axes of the slice: x: 2, y: 2, z: 4, core: 2. Of those that a mesh axis runs over, the one named last changes fastest.
Arguments:
- train_grads: bfloat16 [512, 32768], P('groups', 'docs'), parts along dimension 0, may hold values from -400 to 400, as said below
- query_grads: bfloat16 [600, 32768], P(None, 'docs'), may hold values from -400 to 400, as said below
Outputs:
- scores: float32 [512, 600], P(('groups', 'docs')), parts along dimension 0
There are 2 independent parts, one for each index of `groups`. A program takes and returns all parts, laid end to end along the dimension named above; an argument that names none is the same for every part. Nothing has to cross between parts.
Inputs may be any that keep to these rules, and one draw needn't show every extreme that they name: `train_grads`: finite real values. `query_grads`: finite real values.
All inputs are finite; a program needn't handle non-finite values.
Results may differ from a plain program's by a relative error of at most 0.0003.
Values sent between devices are 32-bit elements; how exact they have to be, the bound alone decides.
No kernel may reach another device: no remote copies, remote signals or barrier semaphores. Data moves between devices by JAX's collectives and lax.ppermute only.
A program may use at most 64 MiB of HBM per device.

v0:
```python
import math

import jax
import jax.numpy as jnp
from jax import lax
from jax.sharding import PartitionSpec as P


def partner(x, axis, distance):
    return lax.ppermute(x, axis, [(i, i ^ 1 << distance) for i in range(lax.axis_size(axis))])


def local(train_grads, query_grads):
    eps = 1e-06
    devices = lax.axis_size("docs")
    layers = devices // 2
    layer_width = 2 * train_grads.shape[1]
    doc_own = jnp.sum(jnp.square(train_grads.astype(jnp.float32)), axis=1)
    query_own = jnp.sum(jnp.square(query_grads.astype(jnp.float32)), axis=1)
    doc_other, query_other = partner((doc_own, query_own), "docs", 0)
    doc_scale = lax.rsqrt(doc_own + doc_other + eps)
    query_scale = lax.rsqrt(query_own + query_other + eps)
    factor = math.sqrt(layer_width / layers)
    dots = lax.dot_general(
        train_grads, query_grads, (((1,), (1,)), ((), ())), preferred_element_type=jnp.float32
    )
    terms = dots * doc_scale[:, None] * query_scale[None, :]
    summed = lax.psum_scatter(terms, "docs", scatter_dimension=0, tiled=True)
    return summed * factor


def solution(mesh):
    in_specs = (P("groups", "docs"), P(None, "docs"))
    out_specs = P(("groups", "docs"), None)
    return jax.shard_map(local, mesh=mesh, in_specs=in_specs, out_specs=out_specs, check_vma=False)
```

profile of v0, /device:TPU:0, one launch (start us, length us, event | category | flops | bytes accessed | tf_op | source)
XLA Modules:
  0.0 81.1 jit_solution(2803704853002911772)
XLA Ops:
  6.5 0.0 copy-start.1
  6.5 0.0 copy-start
  6.5 0.0 reduce-scatter.2.cloned.1.call-start
  6.5 1.7 %multiply_reduce_fusion.1 = f32[256]{0:T(256)S(1)} fusion(bf16[256,2048]{1,0:T(8,128)(2,1)} %param.2), kind=kLoop, calls=%fused_computation.1 | loop fusion | flops 1572608 | bytes 1049600 | tf_op jit(solution)/shard_map/reduce_sum | solution.py:18
  8.2 0.5 collective-permute-start
  8.7 2.3 %multiply_reduce_fusion = f32[600]{0:T(1024)S(1)} fusion(bf16[600,2048]{1,0:T(8,128)(2,1)} %param.3), kind=kLoop, calls=%fused_computation | loop fusion | flops 3685800 | bytes 2460000 | tf_op jit(solution)/shard_map/reduce_sum | solution.py:19
  11.0 0.1 collective-permute-start.1
  11.1 0.0 collective-permute-done
  11.1 1.1 %collective-permute-done.1 = f32[600]{0:T(1024)S(1)} collective-permute-done((f32[600]{0:T(1024)S(1)}, f32[600]{0:T(1024)S(1)}, u32[]{:S(2)}, u32[]{:S(2)}) %collective-permute-start.1) | collective-permute-done | bytes 2432 | tf_op jit(solution)/shard_map/ppermute | solution.py:10
  12.2 0.0 copy-done.1
  12.2 0.0 copy-done
  12.2 1.9 %multiply_multiply_fusion = f32[256,600]{1,0:T(8,128)} fusion(f32[600]{0:T(1024)S(1)} %add_rsqrt_fusion, f32[256]{0:T(256)S(1)} %add_rsqrt_fusion.1, bf16[256,2048]{1,0:T(8,128)(2,1)S(1)} %copy-done.1, bf16[600,2048]{1,0:T(8,128)(2,1)S(1)} %copy-done), kind=kOutput, calls=%fused_computation.2 | convolution fusion | flops 629452800 | bytes 4124000 | tf_op jit(solution)/shard_map/dot_general | solution.py:24
  14.1 0.0 reduce-scatter.2.cloned.1.call-update
  14.1 58.7 %reduce-scatter.2.cloned.1.call-done = f32[16,600]{1,0:T(8,128)} async-done(((f32[256,600]{1,0:T(8,128)}), f32[16,600]{1,0:T(8,128)}) %reduce-scatter.2.cloned.1.call-update) | async-done | bytes 38416 | tf_op jit(solution)/shard_map/reduce_scatter | solution.py:28
  72.8 1.4 %broadcast_multiply_fusion = f32[16,600]{1,0:T(8,128)} fusion(f32[16,600]{1,0:T(8,128)} %reduce-scatter.2.cloned.1.call-done), kind=kLoop, calls=%fused_computation.3 | loop fusion | flops 9600 | bytes 76800 | tf_op jit(solution)/shard_map/mul | solution.py:29
  (2 shorter events, 0.0 us)
Async XLA Ops:
  6.5 5.7 %copy-start.1 = (bf16[256,2048]{1,0:T(8,128)(2,1)S(1)}, bf16[256,2048]{1,0:T(8,128)(2,1)}, u32[]{:S(2)}) copy-start(bf16[256,2048]{1,0:T(8,128)(2,1)} %param.2) | copy-start | bytes 3145732
  6.5 5.7 %copy-start = (bf16[600,2048]{1,0:T(8,128)(2,1)S(1)}, bf16[600,2048]{1,0:T(8,128)(2,1)}, u32[]{:S(2)}) copy-start(bf16[600,2048]{1,0:T(8,128)(2,1)} %param.3) | copy-start | bytes 7372804
  6.5 66.3 %reduce-scatter.2.cloned.1.call-start = ((), (), s32[]{:S(2)}) async-start(), calls=%async_computation.1 | async-start | bytes 696320 | tf_op jit(solution)/shard_map/reduce_scatter | solution.py:28
  8.2 2.9 %collective-permute-start = (f32[256]{0:T(256)S(1)}, f32[256]{0:T(256)S(1)}, u32[]{:S(2)}, u32[]{:S(2)}) collective-permute-start(f32[256]{0:T(256)S(1)} %multiply_reduce_fusion.1), channel_id=1, source_target_pairs={{0,1},{1,0},{2,3},{3,2},{4,5},{5,4},{6,7},{7,6},{8,9},{9,8},{10,11... | collective-permute-start | bytes 3080 | tf_op jit(solution)/shard_map/ppermute | solution.py:10
  11.0 1.2 %collective-permute-start.1 = (f32[600]{0:T(1024)S(1)}, f32[600]{0:T(1024)S(1)}, u32[]{:S(2)}, u32[]{:S(2)}) collective-permute-start(f32[600]{0:T(1024)S(1)} %multiply_reduce_fusion), channel_id=1, source_target_pairs={{0,1},{1,0},{2,3},{3,2},{4,5},{5,4},{6,7},{7,6},{8,9},{9,8},{10,11... | collective-permute-start | bytes 7208 | tf_op jit(solution)/shard_map/ppermute | solution.py:10
Sparse Core Ops, SparseCore 0:
  14.2 58.5 reduce-scatter.1
where the time goes:
time: 81.3 us; the launch traced here: 81.1 us
  waiting for transfers between devices  59.9 us (74%)
  between operations  13.4 us (16%)
  other arithmetic  5.32 us (7%)
  matrix products  1.86 us (2%)
    reduce_scatter x1, waiting for transfers between devices, local(): summed = lax.psum_scatter(terms, 'docs', scatter_dimension=0, tiled=True)  58.7 us
    reduce_sum x1, other arithmetic, local(): query_own = jnp.sum(jnp.square(query_grads.astype(jnp.float32)), axis=1)  2.25 us
    dot_general x1, matrix products, local(): lax.dot_general(train_grads, query_grads, (((1,), (1,)), ((), ())), prefe...  1.86 us
    reduce_sum x1, other arithmetic, local(): doc_own = jnp.sum(jnp.square(train_grads.astype(jnp.float32)), axis=1)  1.66 us
  transfers between devices with their start and end apart: 3, of which 2 were waited for; matrix products, arithmetic and copies ran while one was open for 3% of the time, Pallas kernels for 0%

commit v1 on v0

v1 whole, which is shorter than its diff:
```python
import functools
import math

import jax
import jax.numpy as jnp
from jax import lax
from jax.experimental import pallas as pl
from jax.experimental.pallas import tpu as pltpu
from jax.sharding import PartitionSpec as P

EPS = 1e-06
LANES = 128
CHUNKS = 4


def order(chips, core):
    masks = [1 << b for b in range(chips.bit_length() - 1)]
    if core == 0 and len(masks) > 1:
        masks[0], masks[1] = masks[1], masks[0]
    return masks


def relative(chips, core, slot):
    masks = order(chips, core)
    return sum(m for i, m in enumerate(reversed(masks)) if slot >> i & 1)


def partial_squares(x):
    total = None
    for start in range(0, x.shape[1], LANES):
        part = x[:, start : start + LANES].astype(jnp.float32)
        part = part * part
        total = part if total is None else total + part
    return total


def dots_kernel(chips, train, query, keep, send, train_v, query_v, acc, doc_part, query_part, sem):
    docs, width = train.shape
    queries = query.shape[0]
    rows = docs // (2 * chips)
    step = width // CHUNKS
    me = lax.axis_index("docs")
    core, chip = lax.rem(me, 2), lax.div(me, 2)
    copies = []
    for k in range(CHUNKS):
        cols = pl.ds(k * step, step)
        pair = [
            pltpu.make_async_copy(train.at[:, cols], train_v.at[k], sem.at[k, 0]),
            pltpu.make_async_copy(query.at[:, cols], query_v.at[k], sem.at[k, 1]),
        ]
        for copy in pair:
            copy.start()
        copies.append(pair)
    for k in range(CHUNKS):
        for copy in copies[k]:
            copy.wait()
        a, b = train_v[k], query_v[k]
        dots = lax.dot_general(a, b, (((1,), (1,)), ((), ())), preferred_element_type=jnp.float32)
        if k == 0:
            acc[:, :queries] = dots
            doc_part[...] = partial_squares(a)
            query_part[...] = partial_squares(b)
        else:
            acc[:, :queries] += dots
            doc_part[...] += partial_squares(a)
            query_part[...] += partial_squares(b)
    acc[:, queries : queries + 1] = jnp.sum(doc_part[...], axis=1, keepdims=True)
    query_row = jnp.sum(query_part[...].T, axis=0, keepdims=True)
    half = chips * rows
    for out, owner in ((keep, core), (send, 1 - core)):
        for slot in range(chips):
            rel = jnp.where(owner == 0, relative(chips, 0, slot), relative(chips, 1, slot))
            target = jnp.bitwise_xor(chip, rel)
            start = pl.multiple_of(target * (2 * rows) + owner * rows, rows)
            out[slot * rows : (slot + 1) * rows, : queries + 1] = acc[pl.ds(start, rows), : queries + 1]
        out[half : half + 1, :queries] = query_row


def scale_kernel(factor, queries, keep, got, terms):
    half = terms.shape[0]
    doc = lax.rsqrt(keep[:half, queries : queries + 1] + got[:half, queries : queries + 1] + EPS) * factor
    query = lax.rsqrt(keep[half : half + 1, :queries] + got[half : half + 1, :queries] + EPS)
    terms[...] = (keep[:half, :queries] + got[:half, :queries]) * doc * query


def local(train_grads, query_grads):
    devices = lax.axis_size("docs")
    chips = devices // 2
    docs, width = train_grads.shape
    queries = query_grads.shape[0]
    factor = math.sqrt(2 * width / chips)
    half = docs // 2
    padded = pl.cdiv(queries + 1, LANES) * LANES
    packed = jax.ShapeDtypeStruct((half + 8, padded), jnp.float32)
    step = width // CHUNKS
    keep, send = pl.pallas_call(
        functools.partial(dots_kernel, chips),
        out_shape=[packed, packed],
        in_specs=[pl.BlockSpec(memory_space=pl.ANY)] * 2,
        out_specs=[pl.BlockSpec(memory_space=pltpu.VMEM)] * 2,
        scratch_shapes=[
            pltpu.VMEM((CHUNKS, docs, step), jnp.bfloat16),
            pltpu.VMEM((CHUNKS, queries, step), jnp.bfloat16),
            pltpu.VMEM((docs, padded), jnp.float32),
            pltpu.VMEM((docs, LANES), jnp.float32),
            pltpu.VMEM((queries, LANES), jnp.float32),
            pltpu.SemaphoreType.DMA((CHUNKS, 2)),
        ],
        compiler_params=pltpu.CompilerParams(vmem_limit_bytes=40 * 2**20),
        name="dots",
    )(train_grads, query_grads)
    got = lax.ppermute(send, "docs", [(i, i ^ 1) for i in range(devices)])
    terms = pl.pallas_call(
        functools.partial(scale_kernel, factor, queries),
        out_shape=jax.ShapeDtypeStruct((half, queries), jnp.float32),
        compiler_params=pltpu.CompilerParams(vmem_limit_bytes=40 * 2**20),
        name="scale",
    )(keep, got)
    orders = order(chips, 0), order(chips, 1)
    for masks in zip(*orders):
        middle = terms.shape[0] // 2
        pairs = [(i, i ^ 2 * masks[i % 2]) for i in range(devices)]
        terms = terms[:middle] + lax.ppermute(terms[middle:], "docs", pairs)
    return terms


def solution(mesh):
    in_specs = (P("groups", "docs"), P(None, "docs"))
    out_specs = P(("groups", "docs"), None)
    return jax.shard_map(local, mesh=mesh, in_specs=in_specs, out_specs=out_specs, check_vma=False)
```

time: 81.3 us -> 24 us (0.30)
  waiting for transfers between devices: 59.9 us -> 9.04 us
  between operations: 13.4 us -> 0.05 us
  starting transfers between devices: 0.64 us -> 8.66 us
  other arithmetic: 5.32 us -> 0.65 us
  local copies, waits for them, and re-layouts: 0.01 us -> 2.94 us
  Pallas kernels: 0 us -> 2.47 us
  matrix products: 1.86 us -> 0 us
    reduce_scatter x1 -> x0, waiting for transfers between devices: 58.7 us -> none  [local(): summed = lax.psum_scatter(terms, 'docs', scatter_dimension=0, tiled=True)]
    ppermute x2 -> x4, starting transfers between devices: 0.63 us -> 8.66 us  [the longest x3 8.14 us: local(): terms = terms[:middle] + lax.ppermute(terms[middle:], 'docs', pairs)]
    ppermute x2 -> x4, waiting for transfers between devices: 1.1 us -> 9.04 us  [the longest x3 7.76 us: local(): terms = terms[:middle] + lax.ppermute(terms[middle:], 'docs', pairs)]
    reduce_sum x2 -> x0, other arithmetic: 3.91 us -> none  [the longest x1 2.25 us: local(): query_own = jnp.sum(jnp.square(query_grads.astype(jnp.float32)), axis=1)]
    unnamed x4, local copies, waits for them, and re-layouts: 0.01 us -> 2.92 us
    pallas_call x0 -> x2, Pallas kernels: none -> 2.47 us  [the longest x1 2.37 us: local(): pl.pallas_call(functools.partial(dots_kernel, chips), out_shape=[packed,...]
    dot_general x1 -> x0, matrix products: 1.86 us -> none  [local(): lax.dot_general(train_grads, query_grads, (((1,), (1,)), ((), ())), prefe...]
    mul x1 -> x0, other arithmetic: 1.4 us -> none  [local(): return summed * factor]
  transfers between devices with their start and end apart: 3 -> 4, of which waited for: 2 -> 4; matrix products, arithmetic and copies ran while one was open for 3% -> 0% of each run, Pallas kernels for 0% -> 0%
where the time goes in v1:
time: 24 us; the launch traced here: 23.8 us
  waiting for transfers between devices  9.04 us (38%)
  starting transfers between devices  8.66 us (36%)
  local copies, waits for them, and re-layouts  2.94 us (12%)
  Pallas kernels  2.47 us (10%)
  other arithmetic  0.65 us (3%)
    ppermute x3, starting transfers between devices, local(): terms = terms[:middle] + lax.ppermute(terms[middle:], 'docs', pairs)  8.14 us
    ppermute x3, waiting for transfers between devices, local(): terms = terms[:middle] + lax.ppermute(terms[middle:], 'docs', pairs)  7.76 us
    unnamed x4, local copies, waits for them, and re-layouts  2.92 us
    pallas_call x1, Pallas kernels, local(): pl.pallas_call(functools.partial(dots_kernel, chips), out_shape=[packed,...  2.37 us
    ppermute x1, waiting for transfers between devices, local(): got = lax.ppermute(send, 'docs', [(i, i ^ 1) for i in range(devices)])  1.29 us
    add x3, other arithmetic, local(): terms = terms[:middle] + lax.ppermute(terms[middle:], 'docs', pairs)  0.65 us
    ppermute x1, starting transfers between devices, local(): got = lax.ppermute(send, 'docs', [(i, i ^ 1) for i in range(devices)])  0.52 us
  transfers between devices with their start and end apart: 4, of which 4 were waited for; matrix products, arithmetic and copies ran while one was open for 0% of the time, Pallas kernels for 0%

profile of v1, /device:TPU:0, one launch (start us, length us, event | category | flops | bytes accessed | tf_op | source)
XLA Modules:
  0.0 23.8 jit_solution(10415702994289544633)
XLA Ops:
  0.0 0.0 copy-start
  0.0 1.7 %copy-done = bf16[600,2048]{1,0:T(8,128)(2,1)S(1)} copy-done((bf16[600,2048]{1,0:T(8,128)(2,1)S(1)}, bf16[600,2048]{1,0:T(8,128)(2,1)}, u32[]{:S(2)}) %copy-start) | copy-done | bytes 2457624
  1.7 0.0 copy-start.1
  1.7 1.2 %copy-done.1 = bf16[256,2048]{1,0:T(8,128)(2,1)S(1)} copy-done((bf16[256,2048]{1,0:T(8,128)(2,1)S(1)}, bf16[256,2048]{1,0:T(8,128)(2,1)}, u32[]{:S(2)}) %copy-start.1) | copy-done | bytes 1048600
  2.9 2.4 %dots.1 = (f32[136,640]{1,0:T(8,128)S(1)}, f32[136,640]{1,0:T(8,128)S(1)}) custom-call(bf16[256,2048]{1,0:T(8,128)(2,1)S(1)} %copy-done.1, bf16[600,2048]{1,0:T(8,128)(2,1)S(1)} %copy-done), custom_call_target="tpu_custom_call" | custom-call | tf_op jit(solution)/shard_map/dots/pallas_call | solution.py:96
  5.3 0.5 %collective-permute-start = (f32[136,640]{1,0:T(8,128)S(1)}, f32[136,640]{1,0:T(8,128)S(1)}, u32[]{:S(2)}, u32[]{:S(2)}) collective-permute-start(f32[136,640]{1,0:T(8,128)S(1)} %get-tuple-element.8), channel_id=1, source_target_pairs={{0,1},{1,0},{2,3},{3,2},{4,5},{5,4},{6,7},{7,6},{8,9},{9,8},{10,11... | collective-permute-start | bytes 1044488 | tf_op jit(solution)/shard_map/ppermute | solution.py:112
  5.8 1.3 %collective-permute-done.got = f32[136,640]{1,0:T(8,128)S(1)} collective-permute-done((f32[136,640]{1,0:T(8,128)S(1)}, f32[136,640]{1,0:T(8,128)S(1)}, u32[]{:S(2)}, u32[]{:S(2)}) %collective-permute-start) | collective-permute-done | bytes 348192 | tf_op jit(solution)/shard_map/ppermute | solution.py:112
  7.1 0.1 scale.1
  7.2 3.0 %collective-permute-start.1 = (f32[64,600]{1,0:T(8,128)S(1)}, f32[64,600]{1,0:T(8,128)S(1)}, u32[]{:S(2)}, u32[]{:S(2)}) collective-permute-start(f32[64,600]{1,0:T(8,128)S(1)} %slice.25), channel_id=1, source_target_pairs={{0,4},{1,3},{2,6},{3,1},{4,0},{5,7},{6,2},{7,5},{8,12},{9,11},{10,... | collective-permute-start | bytes 460808 | tf_op jit(solution)/shard_map/ppermute | solution.py:123
  10.2 3.3 %collective-permute-done.1 = f32[64,600]{1,0:T(8,128)S(1)} collective-permute-done((f32[64,600]{1,0:T(8,128)S(1)}, f32[64,600]{1,0:T(8,128)S(1)}, u32[]{:S(2)}, u32[]{:S(2)}) %collective-permute-start.1) | collective-permute-done | bytes 153632 | tf_op jit(solution)/shard_map/ppermute | solution.py:123
  13.6 2.0 %collective-permute-start.2 = (f32[32,600]{1,0:T(8,128)S(1)}, f32[32,600]{1,0:T(8,128)S(1)}, u32[]{:S(2)}, u32[]{:S(2)}) collective-permute-start(f32[32,600]{1,0:T(8,128)S(1)} %slice.27), channel_id=1, source_target_pairs={{0,2},{1,5},{2,0},{3,7},{4,6},{5,1},{6,4},{7,3},{8,10},{9,13},{10,... | collective-permute-start | bytes 230408 | tf_op jit(solution)/shard_map/ppermute | solution.py:123
  15.6 2.5 %collective-permute-done.2 = f32[32,600]{1,0:T(8,128)S(1)} collective-permute-done((f32[32,600]{1,0:T(8,128)S(1)}, f32[32,600]{1,0:T(8,128)S(1)}, u32[]{:S(2)}, u32[]{:S(2)}) %collective-permute-start.2) | collective-permute-done | bytes 76832 | tf_op jit(solution)/shard_map/ppermute | solution.py:123
  18.1 3.1 %collective-permute-start.3 = (f32[16,600]{1,0:T(8,128)S(1)}, f32[16,600]{1,0:T(8,128)S(1)}, u32[]{:S(2)}, u32[]{:S(2)}) collective-permute-start(f32[16,600]{1,0:T(8,128)S(1)} %slice.29), channel_id=1, source_target_pairs={{0,8},{1,9},{2,10},{3,11},{4,12},{5,13},{6,14},{7,15},{8,0},{9,1},... | collective-permute-start | bytes 115208 | tf_op jit(solution)/shard_map/ppermute | solution.py:123
  21.2 2.0 %collective-permute-done.3 = f32[16,600]{1,0:T(8,128)S(1)} collective-permute-done((f32[16,600]{1,0:T(8,128)S(1)}, f32[16,600]{1,0:T(8,128)S(1)}, u32[]{:S(2)}, u32[]{:S(2)}) %collective-permute-start.3) | collective-permute-done | bytes 38432 | tf_op jit(solution)/shard_map/ppermute | solution.py:123
  23.2 0.6 %slice_add_fusion.2 = f32[16,600]{1,0:T(8,128)} fusion(f32[16,600]{1,0:T(8,128)S(1)} %collective-permute-done.3, f32[32,600]{1,0:T(8,128)S(1)} %slice_add_fusion.1), kind=kLoop, calls=%fused_computation.2 | loop fusion | flops 9600 | bytes 115200 | tf_op jit(solution)/shard_map/add | solution.py:123
  (5 shorter events, 0.1 us)
Async XLA Ops:
  0.0 1.7 %copy-start = (bf16[600,2048]{1,0:T(8,128)(2,1)S(1)}, bf16[600,2048]{1,0:T(8,128)(2,1)}, u32[]{:S(2)}) copy-start(bf16[600,2048]{1,0:T(8,128)(2,1)} %query.1) | copy-start | bytes 7372804
  1.7 1.2 %copy-start.1 = (bf16[256,2048]{1,0:T(8,128)(2,1)S(1)}, bf16[256,2048]{1,0:T(8,128)(2,1)}, u32[]{:S(2)}) copy-start(bf16[256,2048]{1,0:T(8,128)(2,1)} %train.1) | copy-start | bytes 3145732
  5.3 1.8 %collective-permute-start = (f32[136,640]{1,0:T(8,128)S(1)}, f32[136,640]{1,0:T(8,128)S(1)}, u32[]{:S(2)}, u32[]{:S(2)}) collective-permute-start(f32[136,640]{1,0:T(8,128)S(1)} %get-tuple-element.8), channel_id=1, source_target_pairs={{0,1},{1,0},{2,3},{3,2},{4,5},{5,4},{6,7},{7,6},{8,9},{9,8},{10,11... | collective-permute-start | bytes 1044488 | tf_op jit(solution)/shard_map/ppermute | solution.py:112
  7.2 6.3 %collective-permute-start.1 = (f32[64,600]{1,0:T(8,128)S(1)}, f32[64,600]{1,0:T(8,128)S(1)}, u32[]{:S(2)}, u32[]{:S(2)}) collective-permute-start(f32[64,600]{1,0:T(8,128)S(1)} %slice.25), channel_id=1, source_target_pairs={{0,4},{1,3},{2,6},{3,1},{4,0},{5,7},{6,2},{7,5},{8,12},{9,11},{10,... | collective-permute-start | bytes 460808 | tf_op jit(solution)/shard_map/ppermute | solution.py:123
  13.6 4.5 %collective-permute-start.2 = (f32[32,600]{1,0:T(8,128)S(1)}, f32[32,600]{1,0:T(8,128)S(1)}, u32[]{:S(2)}, u32[]{:S(2)}) collective-permute-start(f32[32,600]{1,0:T(8,128)S(1)} %slice.27), channel_id=1, source_target_pairs={{0,2},{1,5},{2,0},{3,7},{4,6},{5,1},{6,4},{7,3},{8,10},{9,13},{10,... | collective-permute-start | bytes 230408 | tf_op jit(solution)/shard_map/ppermute | solution.py:123
  18.1 5.1 %collective-permute-start.3 = (f32[16,600]{1,0:T(8,128)S(1)}, f32[16,600]{1,0:T(8,128)S(1)}, u32[]{:S(2)}, u32[]{:S(2)}) collective-permute-start(f32[16,600]{1,0:T(8,128)S(1)} %slice.29), channel_id=1, source_target_pairs={{0,8},{1,9},{2,10},{3,11},{4,12},{5,13},{6,14},{7,15},{8,0},{9,1},... | collective-permute-start | bytes 115208 | tf_op jit(solution)/shard_map/ppermute | solution.py:123

commit v2 on v1

--- a/solution.py
+++ b/solution.py
@@ -13,16 +13,18 @@
 CHUNKS = 4
 
 
-def order(chips, core):
-    masks = [1 << b for b in range(chips.bit_length() - 1)]
-    if core == 0 and len(masks) > 1:
-        masks[0], masks[1] = masks[1], masks[0]
-    return masks
+def phases(chips):
+    bits = chips.bit_length() - 1
+    pairs = [[0, 3 << b, 1 << b, 2 << b] for b in range(0, bits - 1, 2)]
+    return pairs + [[0, 1 << bits - 1]] * (bits % 2)
 
 
-def relative(chips, core, slot):
-    masks = order(chips, core)
-    return sum(m for i, m in enumerate(reversed(masks)) if slot >> i & 1)
+def relative(chips, slot):
+    total = 0
+    for offsets in reversed(phases(chips)):
+        slot, digit = divmod(slot, len(offsets))
+        total ^= offsets[digit]
+    return total
 
 
 def partial_squares(x):
@@ -69,8 +71,7 @@
     half = chips * rows
     for out, owner in ((keep, core), (send, 1 - core)):
         for slot in range(chips):
-            rel = jnp.where(owner == 0, relative(chips, 0, slot), relative(chips, 1, slot))
-            target = jnp.bitwise_xor(chip, rel)
+            target = jnp.bitwise_xor(chip, relative(chips, slot))
             start = pl.multiple_of(target * (2 * rows) + owner * rows, rows)
             out[slot * rows : (slot + 1) * rows, : queries + 1] = acc[pl.ds(start, rows), : queries + 1]
         out[half : half + 1, :queries] = query_row
@@ -96,7 +97,7 @@
     keep, send = pl.pallas_call(
         functools.partial(dots_kernel, chips),
         out_shape=[packed, packed],
-        in_specs=[pl.BlockSpec(memory_space=pl.ANY)] * 2,
+        in_specs=[pl.BlockSpec(memory_space=pltpu.HBM)] * 2,
         out_specs=[pl.BlockSpec(memory_space=pltpu.VMEM)] * 2,
         scratch_shapes=[
             pltpu.VMEM((CHUNKS, docs, step), jnp.bfloat16),
@@ -108,7 +109,7 @@
         ],
         compiler_params=pltpu.CompilerParams(vmem_limit_bytes=40 * 2**20),
         name="dots",
-    )(train_grads, query_grads)
+    )(*(pltpu.with_memory_space_constraint(x, pltpu.HBM) for x in (train_grads, query_grads)))
     got = lax.ppermute(send, "docs", [(i, i ^ 1) for i in range(devices)])
     terms = pl.pallas_call(
         functools.partial(scale_kernel, factor, queries),
@@ -116,11 +117,12 @@
         compiler_params=pltpu.CompilerParams(vmem_limit_bytes=40 * 2**20),
         name="scale",
     )(keep, got)
-    orders = order(chips, 0), order(chips, 1)
-    for masks in zip(*orders):
-        middle = terms.shape[0] // 2
-        pairs = [(i, i ^ 2 * masks[i % 2]) for i in range(devices)]
-        terms = terms[:middle] + lax.ppermute(terms[middle:], "docs", pairs)
+    for offsets in phases(chips):
+        parts = jnp.split(terms, len(offsets))
+        moves = [[(i, i ^ 2 * offset) for i in range(devices)] for offset in offsets]
+        terms = parts[0]
+        for part, pairs in zip(parts[1:], moves[1:]):
+            terms = terms + lax.ppermute(part, "docs", pairs)
     return terms
 
 

time: 24 us -> 19.6 us (0.82)
  local copies, waits for them, and re-layouts: 2.94 us -> 0.02 us
  waiting for transfers between devices: 9.04 us -> 7.84 us
  starting transfers between devices: 8.66 us -> 7.78 us
  Pallas kernels: 2.47 us -> 3.17 us
    unnamed x4 -> x0, local copies, waits for them, and re-layouts: 2.92 us -> none
    ppermute x3 -> x4, waiting for transfers between devices: 7.76 us -> 6.56 us  [local(): terms = terms + lax.ppermute(part, 'docs', pairs)]
    ppermute x3 -> x4, starting transfers between devices: 8.14 us -> 7.27 us  [local(): terms = terms + lax.ppermute(part, 'docs', pairs)]
    pallas_call x1, Pallas kernels: 2.37 us -> 3.06 us  [local(): pl.pallas_call(functools.partial(dots_kernel, chips), out_shape=[packed,...]
    add x3 -> x2, other arithmetic: 0.65 us -> 0.65 us  [local(): terms = terms + lax.ppermute(part, 'docs', pairs)]
  transfers between devices with their start and end apart: 4 -> 5, of which waited for: 4 -> 5; matrix products, arithmetic and copies ran while one was open for 0% -> 0% of each run, Pallas kernels for 0% -> 0%
where the time goes in v2:
time: 19.6 us; the launch traced here: 19.5 us
  waiting for transfers between devices  7.84 us (40%)
  starting transfers between devices  7.78 us (40%)
  Pallas kernels  3.17 us (16%)
  other arithmetic  0.65 us (3%)
    ppermute x4, starting transfers between devices, local(): terms = terms + lax.ppermute(part, 'docs', pairs)  7.27 us
    ppermute x4, waiting for transfers between devices, local(): terms = terms + lax.ppermute(part, 'docs', pairs)  6.56 us
    pallas_call x1, Pallas kernels, local(): pl.pallas_call(functools.partial(dots_kernel, chips), out_shape=[packed,...  3.06 us
    ppermute x1, waiting for transfers between devices, local(): got = lax.ppermute(send, 'docs', [(i, i ^ 1) for i in range(devices)])  1.29 us
    add x2, other arithmetic, local(): terms = terms + lax.ppermute(part, 'docs', pairs)  0.65 us
    ppermute x1, starting transfers between devices, local(): got = lax.ppermute(send, 'docs', [(i, i ^ 1) for i in range(devices)])  0.52 us
  transfers between devices with their start and end apart: 5, of which 5 were waited for; matrix products, arithmetic and copies ran while one was open for 0% of the time, Pallas kernels for 0%

profile of v2, /device:TPU:0, one launch (start us, length us, event | category | flops | bytes accessed | tf_op | source)
XLA Modules:
  0.0 19.5 jit_solution(12783264114301128763)
XLA Ops:
  0.0 3.1 %dots.1 = (f32[136,640]{1,0:T(8,128)S(1)}, f32[136,640]{1,0:T(8,128)S(1)}) custom-call(bf16[256,2048]{1,0:T(8,128)(2,1)} %train.1, bf16[600,2048]{1,0:T(8,128)(2,1)} %query.1), custom_call_target="tpu_custom_call" | custom-call | tf_op jit(solution)/shard_map/dots/pallas_call | solution.py:97
  3.1 0.5 %collective-permute-start = (f32[136,640]{1,0:T(8,128)S(1)}, f32[136,640]{1,0:T(8,128)S(1)}, u32[]{:S(2)}, u32[]{:S(2)}) collective-permute-start(f32[136,640]{1,0:T(8,128)S(1)} %get-tuple-element.8), channel_id=1, source_target_pairs={{0,1},{1,0},{2,3},{3,2},{4,5},{5,4},{6,7},{7,6},{8,9},{9,8},{10,11... | collective-permute-start | bytes 1044488 | tf_op jit(solution)/shard_map/ppermute | solution.py:113
  3.6 1.3 %collective-permute-done.got = f32[136,640]{1,0:T(8,128)S(1)} collective-permute-done((f32[136,640]{1,0:T(8,128)S(1)}, f32[136,640]{1,0:T(8,128)S(1)}, u32[]{:S(2)}, u32[]{:S(2)}) %collective-permute-start) | collective-permute-done | bytes 348192 | tf_op jit(solution)/shard_map/ppermute | solution.py:113
  4.9 0.1 scale.1
  5.0 4.0 %collective-permute-start.1 = (f32[32,600]{1,0:T(8,128)S(1)}, f32[32,600]{1,0:T(8,128)S(1)}, u32[]{:S(2)}, u32[]{:S(2)}) collective-permute-start(f32[32,600]{1,0:T(8,128)S(1)} %get-tuple-element.9), channel_id=1, source_target_pairs={{0,6},{1,7},{2,4},{3,5},{4,2},{5,3},{6,0},{7,1},{8,14},{9,15},{10,... | collective-permute-start | bytes 230408 | tf_op jit(solution)/shard_map/ppermute | solution.py:125
  9.0 0.4 %collective-permute-start.3 = (f32[32,600]{1,0:T(8,128)S(1)}, f32[32,600]{1,0:T(8,128)S(1)}, u32[]{:S(2)}, u32[]{:S(2)}) collective-permute-start(f32[32,600]{1,0:T(8,128)S(1)} %get-tuple-element.10), channel_id=1, source_target_pairs={{0,4},{1,5},{2,6},{3,7},{4,0},{5,1},{6,2},{7,3},{8,12},{9,13},{10,... | collective-permute-start | bytes 230408 | tf_op jit(solution)/shard_map/ppermute | solution.py:125
  9.4 0.2 collective-permute-start.2
  9.6 2.5 %collective-permute-done.1 = f32[32,600]{1,0:T(8,128)S(1)} collective-permute-done((f32[32,600]{1,0:T(8,128)S(1)}, f32[32,600]{1,0:T(8,128)S(1)}, u32[]{:S(2)}, u32[]{:S(2)}) %collective-permute-start.1) | collective-permute-done | bytes 76832 | tf_op jit(solution)/shard_map/ppermute | solution.py:125
  12.1 1.6 %collective-permute-done.3 = f32[32,600]{1,0:T(8,128)S(1)} collective-permute-done((f32[32,600]{1,0:T(8,128)S(1)}, f32[32,600]{1,0:T(8,128)S(1)}, u32[]{:S(2)}, u32[]{:S(2)}) %collective-permute-start.3) | collective-permute-done | bytes 76832 | tf_op jit(solution)/shard_map/ppermute | solution.py:125
  13.6 0.2 %collective-permute-done.2 = f32[32,600]{1,0:T(8,128)S(1)} collective-permute-done((f32[32,600]{1,0:T(8,128)S(1)}, f32[32,600]{1,0:T(8,128)S(1)}, u32[]{:S(2)}, u32[]{:S(2)}) %collective-permute-start.2) | collective-permute-done | bytes 76832 | tf_op jit(solution)/shard_map/ppermute | solution.py:125
  13.9 2.7 %collective-permute-start.4 = (f32[16,600]{1,0:T(8,128)S(1)}, f32[16,600]{1,0:T(8,128)S(1)}, u32[]{:S(2)}, u32[]{:S(2)}) collective-permute-start(f32[16,600]{1,0:T(8,128)S(1)} %split.29), channel_id=1, source_target_pairs={{0,8},{1,9},{2,10},{3,11},{4,12},{5,13},{6,14},{7,15},{8,0},{9,1},... | collective-permute-start | bytes 115208 | tf_op jit(solution)/shard_map/ppermute | solution.py:125
  16.6 2.3 %collective-permute-done.4 = f32[16,600]{1,0:T(8,128)S(1)} collective-permute-done((f32[16,600]{1,0:T(8,128)S(1)}, f32[16,600]{1,0:T(8,128)S(1)}, u32[]{:S(2)}, u32[]{:S(2)}) %collective-permute-start.4) | collective-permute-done | bytes 38432 | tf_op jit(solution)/shard_map/ppermute | solution.py:125
  18.9 0.6 %slice_add_fusion.1 = f32[16,600]{1,0:T(8,128)} fusion(f32[16,600]{1,0:T(8,128)S(1)} %collective-permute-done.4, f32[32,600]{1,0:T(8,128)S(1)} %fusion.1), kind=kLoop, calls=%fused_computation.3 | loop fusion | flops 9600 | bytes 115200 | tf_op jit(solution)/shard_map/add | solution.py:125
  (3 shorter events, 0.0 us)
Async XLA Ops:
  3.1 1.8 %collective-permute-start = (f32[136,640]{1,0:T(8,128)S(1)}, f32[136,640]{1,0:T(8,128)S(1)}, u32[]{:S(2)}, u32[]{:S(2)}) collective-permute-start(f32[136,640]{1,0:T(8,128)S(1)} %get-tuple-element.8), channel_id=1, source_target_pairs={{0,1},{1,0},{2,3},{3,2},{4,5},{5,4},{6,7},{7,6},{8,9},{9,8},{10,11... | collective-permute-start | bytes 1044488 | tf_op jit(solution)/shard_map/ppermute | solution.py:113
  5.0 7.1 %collective-permute-start.1 = (f32[32,600]{1,0:T(8,128)S(1)}, f32[32,600]{1,0:T(8,128)S(1)}, u32[]{:S(2)}, u32[]{:S(2)}) collective-permute-start(f32[32,600]{1,0:T(8,128)S(1)} %get-tuple-element.9), channel_id=1, source_target_pairs={{0,6},{1,7},{2,4},{3,5},{4,2},{5,3},{6,0},{7,1},{8,14},{9,15},{10,... | collective-permute-start | bytes 230408 | tf_op jit(solution)/shard_map/ppermute | solution.py:125
  9.0 4.7 %collective-permute-start.3 = (f32[32,600]{1,0:T(8,128)S(1)}, f32[32,600]{1,0:T(8,128)S(1)}, u32[]{:S(2)}, u32[]{:S(2)}) collective-permute-start(f32[32,600]{1,0:T(8,128)S(1)} %get-tuple-element.10), channel_id=1, source_target_pairs={{0,4},{1,5},{2,6},{3,7},{4,0},{5,1},{6,2},{7,3},{8,12},{9,13},{10,... | collective-permute-start | bytes 230408 | tf_op jit(solution)/shard_map/ppermute | solution.py:125
  9.4 4.4 %collective-permute-start.2 = (f32[32,600]{1,0:T(8,128)S(1)}, f32[32,600]{1,0:T(8,128)S(1)}, u32[]{:S(2)}, u32[]{:S(2)}) collective-permute-start(f32[32,600]{1,0:T(8,128)S(1)} %get-tuple-element.11), channel_id=1, source_target_pairs={{0,2},{1,3},{2,0},{3,1},{4,6},{5,7},{6,4},{7,5},{8,10},{9,11},{10,... | collective-permute-start | bytes 230408 | tf_op jit(solution)/shard_map/ppermute | solution.py:125
  13.9 5.0 %collective-permute-start.4 = (f32[16,600]{1,0:T(8,128)S(1)}, f32[16,600]{1,0:T(8,128)S(1)}, u32[]{:S(2)}, u32[]{:S(2)}) collective-permute-start(f32[16,600]{1,0:T(8,128)S(1)} %split.29), channel_id=1, source_target_pairs={{0,8},{1,9},{2,10},{3,11},{4,12},{5,13},{6,14},{7,15},{8,0},{9,1},... | collective-permute-start | bytes 115208 | tf_op jit(solution)/shard_map/ppermute | solution.py:125

commit v3 on v2

v3 whole, which is shorter than its diff:
```python
import functools
import math

import jax
import jax.numpy as jnp
from jax import lax
from jax.experimental import pallas as pl
from jax.experimental.pallas import tpu as pltpu
from jax.sharding import PartitionSpec as P

EPS = 1e-06
LANES = 128


def phases(chips):
    bits = chips.bit_length() - 1
    pairs = [[0, 3 << b, 1 << b, 2 << b] for b in range(0, bits - 1, 2)]
    return pairs + [[0, 1 << bits - 1]] * (bits % 2)


def relative(chips, slot):
    total = 0
    for offsets in reversed(phases(chips)):
        slot, digit = divmod(slot, len(offsets))
        total ^= offsets[digit]
    return total


def partial_squares(x):
    total = None
    for start in range(0, x.shape[1], LANES):
        part = x[:, start : start + LANES].astype(jnp.float32)
        part = part * part
        total = part if total is None else total + part
    return total


def dots_kernel(chips, cuts, train, query, keep, send, train_v, query_v, doc_part, query_part, sem):
    docs, queries = train.shape[0], query.shape[0]
    half = docs // 2
    rows = half // chips
    me = lax.axis_index("docs")
    core, chip = lax.rem(me, 2), lax.div(me, 2)
    spans = list(zip(cuts[:-1], cuts[1:]))
    copies = []
    for k, (low, high) in enumerate(spans):
        cols = pl.ds(low, high - low)
        pair = [
            pltpu.make_async_copy(train.at[:, cols], train_v.at[:, cols], sem.at[k, 0]),
            pltpu.make_async_copy(query.at[:, cols], query_v.at[:, cols], sem.at[k, 1]),
        ]
        for copy in pair:
            copy.start()
        copies.append(pair)
    starts = []
    for owner in (core, 1 - core):
        for slot in range(chips):
            target = jnp.bitwise_xor(chip, relative(chips, slot))
            starts.append(pl.multiple_of(target * (2 * rows) + owner * rows, rows))
    for k, (low, high) in enumerate(spans):
        for copy in copies[k]:
            copy.wait()
        a = jnp.concatenate([train_v[pl.ds(start, rows), low:high] for start in starts], axis=0)
        b = query_v[:, low:high]
        dots = lax.dot_general(b, a, (((1,), (1,)), ((), ())), preferred_element_type=jnp.float32)
        if k == 0:
            keep[:queries, :] = dots[:, :half]
            send[:queries, :] = dots[:, half:]
            doc_part[...] = partial_squares(a)
            query_part[...] = partial_squares(b)
        else:
            keep[:queries, :] += dots[:, :half]
            send[:queries, :] += dots[:, half:]
            doc_part[...] += partial_squares(a)
            query_part[...] += partial_squares(b)
    doc_row = jnp.sum(doc_part[...].T, axis=0, keepdims=True)
    keep[queries : queries + 1, :] = doc_row[:, :half]
    send[queries : queries + 1, :] = doc_row[:, half:]
    query_row = jnp.sum(query_part[...].T, axis=0, keepdims=True)
    for i, low in enumerate(range(0, queries, half)):
        part = query_row[:, low : low + half]
        for out in (keep, send):
            out[queries + 1 + i : queries + 2 + i, : part.shape[1]] = part


def scale_kernel(factor, queries, keep, got, terms):
    half = keep.shape[1]
    doc = lax.rsqrt(keep[queries : queries + 1, :] + got[queries : queries + 1, :] + EPS) * factor
    parts = []
    for i, low in enumerate(range(0, queries, half)):
        row, width = queries + 1 + i, min(half, queries - low)
        parts.append(keep[row : row + 1, :width] + got[row : row + 1, :width])
    query = lax.rsqrt(jnp.concatenate(parts, axis=1) + EPS)
    terms[...] = ((keep[:queries, :] + got[:queries, :]) * doc).T * query


def local(train_grads, query_grads):
    devices = lax.axis_size("docs")
    chips = devices // 2
    docs, width = train_grads.shape
    queries = query_grads.shape[0]
    factor = math.sqrt(2 * width / chips)
    half = docs // 2
    height = pl.cdiv(queries + 1 + pl.cdiv(queries, half), 8) * 8
    packed = jax.ShapeDtypeStruct((height, half), jnp.float32)
    cuts = [0, width // 4, width * 5 // 8, width]
    keep, send = pl.pallas_call(
        functools.partial(dots_kernel, chips, cuts),
        out_shape=[packed, packed],
        in_specs=[pl.BlockSpec(memory_space=pl.ANY)] * 2,
        out_specs=[pl.BlockSpec(memory_space=pltpu.VMEM)] * 2,
        scratch_shapes=[
            pltpu.VMEM((docs, width), jnp.bfloat16),
            pltpu.VMEM((queries, width), jnp.bfloat16),
            pltpu.VMEM((docs, LANES), jnp.float32),
            pltpu.VMEM((queries, LANES), jnp.float32),
            pltpu.SemaphoreType.DMA((len(cuts) - 1, 2)),
        ],
        compiler_params=pltpu.CompilerParams(vmem_limit_bytes=40 * 2**20),
        name="dots",
    )(*(pltpu.with_memory_space_constraint(x, pltpu.HBM) for x in (train_grads, query_grads)))
    got = lax.ppermute(send, "docs", [(i, i ^ 1) for i in range(devices)])
    terms = pl.pallas_call(
        functools.partial(scale_kernel, factor, queries),
        out_shape=jax.ShapeDtypeStruct((half, queries), jnp.float32),
        compiler_params=pltpu.CompilerParams(vmem_limit_bytes=40 * 2**20),
        name="scale",
    )(keep, got)
    for offsets in phases(chips):
        parts = jnp.split(terms, len(offsets))
        moves = [[(i, i ^ 2 * offset) for i in range(devices)] for offset in offsets]
        terms = parts[0]
        for part, pairs in zip(parts[1:], moves[1:]):
            terms = terms + lax.ppermute(part, "docs", pairs)
    return terms


def solution(mesh):
    in_specs = (P("groups", "docs"), P(None, "docs"))
    out_specs = P(("groups", "docs"), None)
    return jax.shard_map(local, mesh=mesh, in_specs=in_specs, out_specs=out_specs, check_vma=False)
```

time: 19.6 us -> 19.4 us (0.990)
    pallas_call x1, Pallas kernels: 3.06 us -> 2.83 us  [local(): pl.pallas_call(functools.partial(dots_kernel, chips, cuts), out_shape=[pa...]
where the time goes in v3:
time: 19.4 us; the launch traced here: 19.3 us
  waiting for transfers between devices  7.79 us (40%)
  starting transfers between devices  7.78 us (40%)
  Pallas kernels  3.01 us (16%)
  other arithmetic  0.65 us (3%)
    ppermute x4, starting transfers between devices, local(): terms = terms + lax.ppermute(part, 'docs', pairs)  7.26 us
    ppermute x4, waiting for transfers between devices, local(): terms = terms + lax.ppermute(part, 'docs', pairs)  6.56 us
    pallas_call x1, Pallas kernels, local(): pl.pallas_call(functools.partial(dots_kernel, chips, cuts), out_shape=[pa...  2.83 us
    ppermute x1, waiting for transfers between devices, local(): got = lax.ppermute(send, 'docs', [(i, i ^ 1) for i in range(devices)])  1.23 us
    add x2, other arithmetic, local(): terms = terms + lax.ppermute(part, 'docs', pairs)  0.65 us
    ppermute x1, starting transfers between devices, local(): got = lax.ppermute(send, 'docs', [(i, i ^ 1) for i in range(devices)])  0.52 us
  transfers between devices with their start and end apart: 5, of which 5 were waited for; matrix products, arithmetic and copies ran while one was open for 0% of the time, Pallas kernels for 0%

profile of v3, /device:TPU:0, one launch (start us, length us, event | category | flops | bytes accessed | tf_op | source)
XLA Modules:
  0.0 19.3 jit_solution(18197960863221715976)
XLA Ops:
  0.0 2.8 %dots.1 = (f32[608,128]{1,0:T(8,128)S(1)}, f32[608,128]{1,0:T(8,128)S(1)}) custom-call(bf16[256,2048]{1,0:T(8,128)(2,1)} %train.1, bf16[600,2048]{1,0:T(8,128)(2,1)} %query.1), custom_call_target="tpu_custom_call" | custom-call | tf_op jit(solution)/shard_map/dots/pallas_call | solution.py:107
  2.8 0.5 %collective-permute-start = (f32[608,128]{1,0:T(8,128)S(1)}, f32[608,128]{1,0:T(8,128)S(1)}, u32[]{:S(2)}, u32[]{:S(2)}) collective-permute-start(f32[608,128]{1,0:T(8,128)S(1)} %get-tuple-element.8), channel_id=1, source_target_pairs={{0,1},{1,0},{2,3},{3,2},{4,5},{5,4},{6,7},{7,6},{8,9},{9,8},{10,11... | collective-permute-start | bytes 933896 | tf_op jit(solution)/shard_map/ppermute | solution.py:122
  3.4 1.2 %collective-permute-done.got = f32[608,128]{1,0:T(8,128)S(1)} collective-permute-done((f32[608,128]{1,0:T(8,128)S(1)}, f32[608,128]{1,0:T(8,128)S(1)}, u32[]{:S(2)}, u32[]{:S(2)}) %collective-permute-start) | collective-permute-done | bytes 311328 | tf_op jit(solution)/shard_map/ppermute | solution.py:122
  4.6 0.2 scale.1
  4.8 4.0 %collective-permute-start.1 = (f32[32,600]{1,0:T(8,128)S(1)}, f32[32,600]{1,0:T(8,128)S(1)}, u32[]{:S(2)}, u32[]{:S(2)}) collective-permute-start(f32[32,600]{1,0:T(8,128)S(1)} %get-tuple-element.9), channel_id=1, source_target_pairs={{0,6},{1,7},{2,4},{3,5},{4,2},{5,3},{6,0},{7,1},{8,14},{9,15},{10,... | collective-permute-start | bytes 230408 | tf_op jit(solution)/shard_map/ppermute | solution.py:134
  8.8 0.4 %collective-permute-start.3 = (f32[32,600]{1,0:T(8,128)S(1)}, f32[32,600]{1,0:T(8,128)S(1)}, u32[]{:S(2)}, u32[]{:S(2)}) collective-permute-start(f32[32,600]{1,0:T(8,128)S(1)} %get-tuple-element.10), channel_id=1, source_target_pairs={{0,4},{1,5},{2,6},{3,7},{4,0},{5,1},{6,2},{7,3},{8,12},{9,13},{10,... | collective-permute-start | bytes 230408 | tf_op jit(solution)/shard_map/ppermute | solution.py:134
  9.2 0.2 collective-permute-start.2
  9.4 2.5 %collective-permute-done.1 = f32[32,600]{1,0:T(8,128)S(1)} collective-permute-done((f32[32,600]{1,0:T(8,128)S(1)}, f32[32,600]{1,0:T(8,128)S(1)}, u32[]{:S(2)}, u32[]{:S(2)}) %collective-permute-start.1) | collective-permute-done | bytes 76832 | tf_op jit(solution)/shard_map/ppermute | solution.py:134
  11.9 1.5 %collective-permute-done.3 = f32[32,600]{1,0:T(8,128)S(1)} collective-permute-done((f32[32,600]{1,0:T(8,128)S(1)}, f32[32,600]{1,0:T(8,128)S(1)}, u32[]{:S(2)}, u32[]{:S(2)}) %collective-permute-start.3) | collective-permute-done | bytes 76832 | tf_op jit(solution)/shard_map/ppermute | solution.py:134
  13.4 0.2 %collective-permute-done.2 = f32[32,600]{1,0:T(8,128)S(1)} collective-permute-done((f32[32,600]{1,0:T(8,128)S(1)}, f32[32,600]{1,0:T(8,128)S(1)}, u32[]{:S(2)}, u32[]{:S(2)}) %collective-permute-start.2) | collective-permute-done | bytes 76832 | tf_op jit(solution)/shard_map/ppermute | solution.py:134
  13.7 2.7 %collective-permute-start.4 = (f32[16,600]{1,0:T(8,128)S(1)}, f32[16,600]{1,0:T(8,128)S(1)}, u32[]{:S(2)}, u32[]{:S(2)}) collective-permute-start(f32[16,600]{1,0:T(8,128)S(1)} %split.29), channel_id=1, source_target_pairs={{0,8},{1,9},{2,10},{3,11},{4,12},{5,13},{6,14},{7,15},{8,0},{9,1},... | collective-permute-start | bytes 115208 | tf_op jit(solution)/shard_map/ppermute | solution.py:134
  16.3 2.3 %collective-permute-done.4 = f32[16,600]{1,0:T(8,128)S(1)} collective-permute-done((f32[16,600]{1,0:T(8,128)S(1)}, f32[16,600]{1,0:T(8,128)S(1)}, u32[]{:S(2)}, u32[]{:S(2)}) %collective-permute-start.4) | collective-permute-done | bytes 38432 | tf_op jit(solution)/shard_map/ppermute | solution.py:134
  18.7 0.6 %slice_add_fusion.1 = f32[16,600]{1,0:T(8,128)} fusion(f32[16,600]{1,0:T(8,128)S(1)} %collective-permute-done.4, f32[32,600]{1,0:T(8,128)S(1)} %fusion.1), kind=kLoop, calls=%fused_computation.3 | loop fusion | flops 9600 | bytes 115200 | tf_op jit(solution)/shard_map/add | solution.py:134
  (3 shorter events, 0.0 us)
Async XLA Ops:
  2.8 1.7 %collective-permute-start = (f32[608,128]{1,0:T(8,128)S(1)}, f32[608,128]{1,0:T(8,128)S(1)}, u32[]{:S(2)}, u32[]{:S(2)}) collective-permute-start(f32[608,128]{1,0:T(8,128)S(1)} %get-tuple-element.8), channel_id=1, source_target_pairs={{0,1},{1,0},{2,3},{3,2},{4,5},{5,4},{6,7},{7,6},{8,9},{9,8},{10,11... | collective-permute-start | bytes 933896 | tf_op jit(solution)/shard_map/ppermute | solution.py:122
  4.8 7.1 %collective-permute-start.1 = (f32[32,600]{1,0:T(8,128)S(1)}, f32[32,600]{1,0:T(8,128)S(1)}, u32[]{:S(2)}, u32[]{:S(2)}) collective-permute-start(f32[32,600]{1,0:T(8,128)S(1)} %get-tuple-element.9), channel_id=1, source_target_pairs={{0,6},{1,7},{2,4},{3,5},{4,2},{5,3},{6,0},{7,1},{8,14},{9,15},{10,... | collective-permute-start | bytes 230408 | tf_op jit(solution)/shard_map/ppermute | solution.py:134
  8.8 4.7 %collective-permute-start.3 = (f32[32,600]{1,0:T(8,128)S(1)}, f32[32,600]{1,0:T(8,128)S(1)}, u32[]{:S(2)}, u32[]{:S(2)}) collective-permute-start(f32[32,600]{1,0:T(8,128)S(1)} %get-tuple-element.10), channel_id=1, source_target_pairs={{0,4},{1,5},{2,6},{3,7},{4,0},{5,1},{6,2},{7,3},{8,12},{9,13},{10,... | collective-permute-start | bytes 230408 | tf_op jit(solution)/shard_map/ppermute | solution.py:134
  9.2 4.4 %collective-permute-start.2 = (f32[32,600]{1,0:T(8,128)S(1)}, f32[32,600]{1,0:T(8,128)S(1)}, u32[]{:S(2)}, u32[]{:S(2)}) collective-permute-start(f32[32,600]{1,0:T(8,128)S(1)} %get-tuple-element.11), channel_id=1, source_target_pairs={{0,2},{1,3},{2,0},{3,1},{4,6},{5,7},{6,4},{7,5},{8,10},{9,11},{10,... | collective-permute-start | bytes 230408 | tf_op jit(solution)/shard_map/ppermute | solution.py:134
  13.7 5.0 %collective-permute-start.4 = (f32[16,600]{1,0:T(8,128)S(1)}, f32[16,600]{1,0:T(8,128)S(1)}, u32[]{:S(2)}, u32[]{:S(2)}) collective-permute-start(f32[16,600]{1,0:T(8,128)S(1)} %split.29), channel_id=1, source_target_pairs={{0,8},{1,9},{2,10},{3,11},{4,12},{5,13},{6,14},{7,15},{8,0},{9,1},... | collective-permute-start | bytes 115208 | tf_op jit(solution)/shard_map/ppermute | solution.py:134

commit v4 on v3

--- a/solution.py
+++ b/solution.py
@@ -52,6 +52,7 @@
         for copy in pair:
             copy.start()
         copies.append(pair)
+    middle = pl.cdiv(queries, 32) * 16
     starts = []
     for owner in (core, 1 - core):
         for slot in range(chips):
@@ -62,17 +63,21 @@
             copy.wait()
         a = jnp.concatenate([train_v[pl.ds(start, rows), low:high] for start in starts], axis=0)
         b = query_v[:, low:high]
-        dots = lax.dot_general(b, a, (((1,), (1,)), ((), ())), preferred_element_type=jnp.float32)
+        for first, end in ((0, middle), (middle, queries)):
+            dots = lax.dot_general(b[first:end], a, (((1,), (1,)), ((), ())), preferred_element_type=jnp.float32)
+            squares = partial_squares(b[first:end])
+            if k == 0:
+                keep[first:end, :] = dots[:, :half]
+                send[first:end, :] = dots[:, half:]
+                query_part[first:end, :] = squares
+            else:
+                keep[first:end, :] += dots[:, :half]
+                send[first:end, :] += dots[:, half:]
+                query_part[first:end, :] += squares
         if k == 0:
-            keep[:queries, :] = dots[:, :half]
-            send[:queries, :] = dots[:, half:]
             doc_part[...] = partial_squares(a)
-            query_part[...] = partial_squares(b)
         else:
-            keep[:queries, :] += dots[:, :half]
-            send[:queries, :] += dots[:, half:]
             doc_part[...] += partial_squares(a)
-            query_part[...] += partial_squares(b)
     doc_row = jnp.sum(doc_part[...].T, axis=0, keepdims=True)
     keep[queries : queries + 1, :] = doc_row[:, :half]
     send[queries : queries + 1, :] = doc_row[:, half:]

time: 19.4 us -> 19.1 us (0.985)
  Pallas kernels: 3.01 us -> 2.66 us
    pallas_call x1, Pallas kernels: 2.83 us -> 2.49 us  [local(): pl.pallas_call(functools.partial(dots_kernel, chips, cuts), out_shape=[pa...]
where the time goes in v4:
time: 19.1 us; the launch traced here: 18.9 us
  waiting for transfers between devices  7.79 us (41%)
  starting transfers between devices  7.78 us (41%)
  Pallas kernels  2.66 us (14%)
  other arithmetic  0.65 us (3%)
    ppermute x4, starting transfers between devices, local(): terms = terms + lax.ppermute(part, 'docs', pairs)  7.26 us
    ppermute x4, waiting for transfers between devices, local(): terms = terms + lax.ppermute(part, 'docs', pairs)  6.56 us
    pallas_call x1, Pallas kernels, local(): pl.pallas_call(functools.partial(dots_kernel, chips, cuts), out_shape=[pa...  2.49 us
    ppermute x1, waiting for transfers between devices, local(): got = lax.ppermute(send, 'docs', [(i, i ^ 1) for i in range(devices)])  1.23 us
    add x2, other arithmetic, local(): terms = terms + lax.ppermute(part, 'docs', pairs)  0.65 us
    ppermute x1, starting transfers between devices, local(): got = lax.ppermute(send, 'docs', [(i, i ^ 1) for i in range(devices)])  0.52 us
  transfers between devices with their start and end apart: 5, of which 5 were waited for; matrix products, arithmetic and copies ran while one was open for 0% of the time, Pallas kernels for 0%

profile of v4, /device:TPU:0, one launch (start us, length us, event | category | flops | bytes accessed | tf_op | source)
XLA Modules:
  0.0 18.9 jit_solution(10097923574177318040)
XLA Ops:
  0.0 2.5 %dots.1 = (f32[608,128]{1,0:T(8,128)S(1)}, f32[608,128]{1,0:T(8,128)S(1)}) custom-call(bf16[256,2048]{1,0:T(8,128)(2,1)} %train.1, bf16[600,2048]{1,0:T(8,128)(2,1)} %query.1), custom_call_target="tpu_custom_call" | custom-call | tf_op jit(solution)/shard_map/dots/pallas_call | solution.py:112
  2.5 0.5 %collective-permute-start = (f32[608,128]{1,0:T(8,128)S(1)}, f32[608,128]{1,0:T(8,128)S(1)}, u32[]{:S(2)}, u32[]{:S(2)}) collective-permute-start(f32[608,128]{1,0:T(8,128)S(1)} %get-tuple-element.8), channel_id=1, source_target_pairs={{0,1},{1,0},{2,3},{3,2},{4,5},{5,4},{6,7},{7,6},{8,9},{9,8},{10,11... | collective-permute-start | bytes 933896 | tf_op jit(solution)/shard_map/ppermute | solution.py:127
  3.0 1.2 %collective-permute-done.got = f32[608,128]{1,0:T(8,128)S(1)} collective-permute-done((f32[608,128]{1,0:T(8,128)S(1)}, f32[608,128]{1,0:T(8,128)S(1)}, u32[]{:S(2)}, u32[]{:S(2)}) %collective-permute-start) | collective-permute-done | bytes 311328 | tf_op jit(solution)/shard_map/ppermute | solution.py:127
  4.2 0.2 scale.1
  4.5 4.0 %collective-permute-start.1 = (f32[32,600]{1,0:T(8,128)S(1)}, f32[32,600]{1,0:T(8,128)S(1)}, u32[]{:S(2)}, u32[]{:S(2)}) collective-permute-start(f32[32,600]{1,0:T(8,128)S(1)} %get-tuple-element.9), channel_id=1, source_target_pairs={{0,6},{1,7},{2,4},{3,5},{4,2},{5,3},{6,0},{7,1},{8,14},{9,15},{10,... | collective-permute-start | bytes 230408 | tf_op jit(solution)/shard_map/ppermute | solution.py:139
  8.4 0.4 %collective-permute-start.3 = (f32[32,600]{1,0:T(8,128)S(1)}, f32[32,600]{1,0:T(8,128)S(1)}, u32[]{:S(2)}, u32[]{:S(2)}) collective-permute-start(f32[32,600]{1,0:T(8,128)S(1)} %get-tuple-element.10), channel_id=1, source_target_pairs={{0,4},{1,5},{2,6},{3,7},{4,0},{5,1},{6,2},{7,3},{8,12},{9,13},{10,... | collective-permute-start | bytes 230408 | tf_op jit(solution)/shard_map/ppermute | solution.py:139
  8.9 0.2 %collective-permute-start.2 = (f32[32,600]{1,0:T(8,128)S(1)}, f32[32,600]{1,0:T(8,128)S(1)}, u32[]{:S(2)}, u32[]{:S(2)}) collective-permute-start(f32[32,600]{1,0:T(8,128)S(1)} %get-tuple-element.11), channel_id=1, source_target_pairs={{0,2},{1,3},{2,0},{3,1},{4,6},{5,7},{6,4},{7,5},{8,10},{9,11},{10,... | collective-permute-start | bytes 230408 | tf_op jit(solution)/shard_map/ppermute | solution.py:139
  9.1 2.5 %collective-permute-done.1 = f32[32,600]{1,0:T(8,128)S(1)} collective-permute-done((f32[32,600]{1,0:T(8,128)S(1)}, f32[32,600]{1,0:T(8,128)S(1)}, u32[]{:S(2)}, u32[]{:S(2)}) %collective-permute-start.1) | collective-permute-done | bytes 76832 | tf_op jit(solution)/shard_map/ppermute | solution.py:139
  11.5 1.6 %collective-permute-done.3 = f32[32,600]{1,0:T(8,128)S(1)} collective-permute-done((f32[32,600]{1,0:T(8,128)S(1)}, f32[32,600]{1,0:T(8,128)S(1)}, u32[]{:S(2)}, u32[]{:S(2)}) %collective-permute-start.3) | collective-permute-done | bytes 76832 | tf_op jit(solution)/shard_map/ppermute | solution.py:139
  13.1 0.2 %collective-permute-done.2 = f32[32,600]{1,0:T(8,128)S(1)} collective-permute-done((f32[32,600]{1,0:T(8,128)S(1)}, f32[32,600]{1,0:T(8,128)S(1)}, u32[]{:S(2)}, u32[]{:S(2)}) %collective-permute-start.2) | collective-permute-done | bytes 76832 | tf_op jit(solution)/shard_map/ppermute | solution.py:139
  13.3 2.7 %collective-permute-start.4 = (f32[16,600]{1,0:T(8,128)S(1)}, f32[16,600]{1,0:T(8,128)S(1)}, u32[]{:S(2)}, u32[]{:S(2)}) collective-permute-start(f32[16,600]{1,0:T(8,128)S(1)} %split.29), channel_id=1, source_target_pairs={{0,8},{1,9},{2,10},{3,11},{4,12},{5,13},{6,14},{7,15},{8,0},{9,1},... | collective-permute-start | bytes 115208 | tf_op jit(solution)/shard_map/ppermute | solution.py:139
  16.0 2.3 %collective-permute-done.4 = f32[16,600]{1,0:T(8,128)S(1)} collective-permute-done((f32[16,600]{1,0:T(8,128)S(1)}, f32[16,600]{1,0:T(8,128)S(1)}, u32[]{:S(2)}, u32[]{:S(2)}) %collective-permute-start.4) | collective-permute-done | bytes 38432 | tf_op jit(solution)/shard_map/ppermute | solution.py:139
  18.3 0.6 %slice_add_fusion.1 = f32[16,600]{1,0:T(8,128)} fusion(f32[16,600]{1,0:T(8,128)S(1)} %collective-permute-done.4, f32[32,600]{1,0:T(8,128)S(1)} %fusion.1), kind=kLoop, calls=%fused_computation.3 | loop fusion | flops 9600 | bytes 115200 | tf_op jit(solution)/shard_map/add | solution.py:139
  (3 shorter events, 0.0 us)
Async XLA Ops:
  2.5 1.8 %collective-permute-start = (f32[608,128]{1,0:T(8,128)S(1)}, f32[608,128]{1,0:T(8,128)S(1)}, u32[]{:S(2)}, u32[]{:S(2)}) collective-permute-start(f32[608,128]{1,0:T(8,128)S(1)} %get-tuple-element.8), channel_id=1, source_target_pairs={{0,1},{1,0},{2,3},{3,2},{4,5},{5,4},{6,7},{7,6},{8,9},{9,8},{10,11... | collective-permute-start | bytes 933896 | tf_op jit(solution)/shard_map/ppermute | solution.py:127
  4.5 7.1 %collective-permute-start.1 = (f32[32,600]{1,0:T(8,128)S(1)}, f32[32,600]{1,0:T(8,128)S(1)}, u32[]{:S(2)}, u32[]{:S(2)}) collective-permute-start(f32[32,600]{1,0:T(8,128)S(1)} %get-tuple-element.9), channel_id=1, source_target_pairs={{0,6},{1,7},{2,4},{3,5},{4,2},{5,3},{6,0},{7,1},{8,14},{9,15},{10,... | collective-permute-start | bytes 230408 | tf_op jit(solution)/shard_map/ppermute | solution.py:139
  8.4 4.7 %collective-permute-start.3 = (f32[32,600]{1,0:T(8,128)S(1)}, f32[32,600]{1,0:T(8,128)S(1)}, u32[]{:S(2)}, u32[]{:S(2)}) collective-permute-start(f32[32,600]{1,0:T(8,128)S(1)} %get-tuple-element.10), channel_id=1, source_target_pairs={{0,4},{1,5},{2,6},{3,7},{4,0},{5,1},{6,2},{7,3},{8,12},{9,13},{10,... | collective-permute-start | bytes 230408 | tf_op jit(solution)/shard_map/ppermute | solution.py:139
  8.9 4.4 %collective-permute-start.2 = (f32[32,600]{1,0:T(8,128)S(1)}, f32[32,600]{1,0:T(8,128)S(1)}, u32[]{:S(2)}, u32[]{:S(2)}) collective-permute-start(f32[32,600]{1,0:T(8,128)S(1)} %get-tuple-element.11), channel_id=1, source_target_pairs={{0,2},{1,3},{2,0},{3,1},{4,6},{5,7},{6,4},{7,5},{8,10},{9,11},{10,... | collective-permute-start | bytes 230408 | tf_op jit(solution)/shard_map/ppermute | solution.py:139
  13.3 5.0 %collective-permute-start.4 = (f32[16,600]{1,0:T(8,128)S(1)}, f32[16,600]{1,0:T(8,128)S(1)}, u32[]{:S(2)}, u32[]{:S(2)}) collective-permute-start(f32[16,600]{1,0:T(8,128)S(1)} %split.29), channel_id=1, source_target_pairs={{0,8},{1,9},{2,10},{3,11},{4,12},{5,13},{6,14},{7,15},{8,0},{9,1},... | collective-permute-start | bytes 115208 | tf_op jit(solution)/shard_map/ppermute | solution.py:139

commit v5 on v4

--- a/solution.py
+++ b/solution.py
@@ -14,16 +14,18 @@
 
 def phases(chips):
     bits = chips.bit_length() - 1
-    pairs = [[0, 3 << b, 1 << b, 2 << b] for b in range(0, bits - 1, 2)]
-    return pairs + [[0, 1 << bits - 1]] * (bits % 2)
+    fours = [(2 << b, [(0, 0), (2 << b, 3 << b), (3 << b, 2 << b), (1 << b, 1 << b)]) for b in range(0, bits - 1, 2)]
+    last = 1 << bits - 1
+    return fours + [(last, [(0, 0), (last, last)])] * (bits % 2)
 
 
-def relative(chips, slot):
-    total = 0
-    for offsets in reversed(phases(chips)):
+def owner_of(chips, chip, slot):
+    result = chip
+    for mask, offsets in reversed(phases(chips)):
         slot, digit = divmod(slot, len(offsets))
-        total ^= offsets[digit]
-    return total
+        clear, marked = offsets[digit]
+        result = jnp.bitwise_xor(result, jnp.where(jnp.bitwise_and(chip, mask) == 0, clear, marked))
+    return result
 
 
 def partial_squares(x):
@@ -56,8 +58,7 @@
     starts = []
     for owner in (core, 1 - core):
         for slot in range(chips):
-            target = jnp.bitwise_xor(chip, relative(chips, slot))
-            starts.append(pl.multiple_of(target * (2 * rows) + owner * rows, rows))
+            starts.append(pl.multiple_of(owner_of(chips, chip, slot) * (2 * rows) + owner * rows, rows))
     for k, (low, high) in enumerate(spans):
         for copy in copies[k]:
             copy.wait()
@@ -88,7 +89,7 @@
             out[queries + 1 + i : queries + 2 + i, : part.shape[1]] = part
 
 
-def scale_kernel(factor, queries, keep, got, terms):
+def scale_kernel(factor, queries, keep, got, *terms):
     half = keep.shape[1]
     doc = lax.rsqrt(keep[queries : queries + 1, :] + got[queries : queries + 1, :] + EPS) * factor
     parts = []
@@ -96,7 +97,10 @@
         row, width = queries + 1 + i, min(half, queries - low)
         parts.append(keep[row : row + 1, :width] + got[row : row + 1, :width])
     query = lax.rsqrt(jnp.concatenate(parts, axis=1) + EPS)
-    terms[...] = ((keep[:queries, :] + got[:queries, :]) * doc).T * query
+    total = ((keep[:queries, :] + got[:queries, :]) * doc).T * query
+    size = terms[0].shape[0]
+    for i, part in enumerate(terms):
+        part[...] = total[i * size : (i + 1) * size, :]
 
 
 def local(train_grads, query_grads):
@@ -125,17 +129,20 @@
         name="dots",
     )(*(pltpu.with_memory_space_constraint(x, pltpu.HBM) for x in (train_grads, query_grads)))
     got = lax.ppermute(send, "docs", [(i, i ^ 1) for i in range(devices)])
-    terms = pl.pallas_call(
+    exchanges = phases(chips)
+    count = len(exchanges[0][1])
+    parts = pl.pallas_call(
         functools.partial(scale_kernel, factor, queries),
-        out_shape=jax.ShapeDtypeStruct((half, queries), jnp.float32),
+        out_shape=[jax.ShapeDtypeStruct((half // count, queries), jnp.float32)] * count,
         compiler_params=pltpu.CompilerParams(vmem_limit_bytes=40 * 2**20),
         name="scale",
     )(keep, got)
-    for offsets in phases(chips):
-        parts = jnp.split(terms, len(offsets))
-        moves = [[(i, i ^ 2 * offset) for i in range(devices)] for offset in offsets]
+    for i, (mask, offsets) in enumerate(exchanges):
+        if i > 0:
+            parts = jnp.split(terms, len(offsets))
         terms = parts[0]
-        for part, pairs in zip(parts[1:], moves[1:]):
+        for part, (clear, marked) in zip(parts[1:], offsets[1:]):
+            pairs = [(d, d ^ 2 * (marked if d // 2 & mask else clear)) for d in range(devices)]
             terms = terms + lax.ppermute(part, "docs", pairs)
     return terms
 

time: 19.1 us -> 18.8 us (0.984)
  waiting for transfers between devices: 7.79 us -> 6.13 us
  starting transfers between devices: 7.78 us -> 9.2 us
    ppermute x4, waiting for transfers between devices: 6.56 us -> 4.9 us  [local(): terms = terms + lax.ppermute(part, 'docs', pairs)]
    ppermute x4, starting transfers between devices: 7.26 us -> 8.68 us  [local(): terms = terms + lax.ppermute(part, 'docs', pairs)]
  transfers between devices with their start and end apart: 5 -> 5, of which waited for: 5 -> 4; matrix products, arithmetic and copies ran while one was open for 0% -> 0% of each run, Pallas kernels for 0% -> 0%
where the time goes in v5:
time: 18.8 us; the launch traced here: 18.7 us
  starting transfers between devices  9.2 us (49%)
  waiting for transfers between devices  6.13 us (33%)
  Pallas kernels  2.66 us (14%)
  other arithmetic  0.64 us (3%)
    ppermute x4, starting transfers between devices, local(): terms = terms + lax.ppermute(part, 'docs', pairs)  8.68 us
    ppermute x4, waiting for transfers between devices, local(): terms = terms + lax.ppermute(part, 'docs', pairs)  4.9 us
    pallas_call x1, Pallas kernels, local(): pl.pallas_call(functools.partial(dots_kernel, chips, cuts), out_shape=[pa...  2.49 us
    ppermute x1, waiting for transfers between devices, local(): got = lax.ppermute(send, 'docs', [(i, i ^ 1) for i in range(devices)])  1.23 us
    add x2, other arithmetic, local(): terms = terms + lax.ppermute(part, 'docs', pairs)  0.64 us
    ppermute x1, starting transfers between devices, local(): got = lax.ppermute(send, 'docs', [(i, i ^ 1) for i in range(devices)])  0.52 us
  transfers between devices with their start and end apart: 5, of which 4 were waited for; matrix products, arithmetic and copies ran while one was open for 0% of the time, Pallas kernels for 0%

profile of v5, /device:TPU:0, one launch (start us, length us, event | category | flops | bytes accessed | tf_op | source)
XLA Modules:
  0.0 18.7 jit_solution(14777946129081588967)
XLA Ops:
  0.0 2.5 %dots.1 = (f32[608,128]{1,0:T(8,128)S(1)}, f32[608,128]{1,0:T(8,128)S(1)}) custom-call(bf16[256,2048]{1,0:T(8,128)(2,1)} %train.1, bf16[600,2048]{1,0:T(8,128)(2,1)} %query.1), custom_call_target="tpu_custom_call" | custom-call | tf_op jit(solution)/shard_map/dots/pallas_call | solution.py:116
  2.5 0.5 %collective-permute-start = (f32[608,128]{1,0:T(8,128)S(1)}, f32[608,128]{1,0:T(8,128)S(1)}, u32[]{:S(2)}, u32[]{:S(2)}) collective-permute-start(f32[608,128]{1,0:T(8,128)S(1)} %get-tuple-element.12), channel_id=1, source_target_pairs={{0,1},{1,0},{2,3},{3,2},{4,5},{5,4},{6,7},{7,6},{8,9},{9,8},{10,11... | collective-permute-start | bytes 933896 | tf_op jit(solution)/shard_map/ppermute | solution.py:131
  3.0 1.2 %collective-permute-done.got = f32[608,128]{1,0:T(8,128)S(1)} collective-permute-done((f32[608,128]{1,0:T(8,128)S(1)}, f32[608,128]{1,0:T(8,128)S(1)}, u32[]{:S(2)}, u32[]{:S(2)}) %collective-permute-start) | collective-permute-done | bytes 311328 | tf_op jit(solution)/shard_map/ppermute | solution.py:131
  4.2 0.2 scale.1
  4.4 3.0 %collective-permute-start.1 = (f32[32,600]{1,0:T(8,128)S(1)}, f32[32,600]{1,0:T(8,128)S(1)}, u32[]{:S(2)}, u32[]{:S(2)}) collective-permute-start(f32[32,600]{1,0:T(8,128)S(1)} %get-tuple-element.14), channel_id=1, source_target_pairs={{0,4},{1,5},{2,6},{3,7},{4,2},{5,3},{6,0},{7,1},{8,12},{9,13},{10,... | collective-permute-start | bytes 230408 | tf_op jit(solution)/shard_map/ppermute | solution.py:146
  7.4 1.0 %collective-permute-start.2 = (f32[32,600]{1,0:T(8,128)S(1)}, f32[32,600]{1,0:T(8,128)S(1)}, u32[]{:S(2)}, u32[]{:S(2)}) collective-permute-start(f32[32,600]{1,0:T(8,128)S(1)} %get-tuple-element.15), channel_id=1, source_target_pairs={{0,6},{1,7},{2,4},{3,5},{4,0},{5,1},{6,2},{7,3},{8,14},{9,15},{10,... | collective-permute-start | bytes 230408 | tf_op jit(solution)/shard_map/ppermute | solution.py:146
  8.4 1.8 %collective-permute-start.3 = (f32[32,600]{1,0:T(8,128)S(1)}, f32[32,600]{1,0:T(8,128)S(1)}, u32[]{:S(2)}, u32[]{:S(2)}) collective-permute-start(f32[32,600]{1,0:T(8,128)S(1)} %get-tuple-element.16), channel_id=1, source_target_pairs={{0,2},{1,3},{2,0},{3,1},{4,6},{5,7},{6,4},{7,5},{8,10},{9,11},{10,... | collective-permute-start | bytes 230408 | tf_op jit(solution)/shard_map/ppermute | solution.py:146
  10.3 1.1 %collective-permute-done.1 = f32[32,600]{1,0:T(8,128)S(1)} collective-permute-done((f32[32,600]{1,0:T(8,128)S(1)}, f32[32,600]{1,0:T(8,128)S(1)}, u32[]{:S(2)}, u32[]{:S(2)}) %collective-permute-start.1) | collective-permute-done | bytes 76832 | tf_op jit(solution)/shard_map/ppermute | solution.py:146
  11.4 1.6 %collective-permute-done.2 = f32[32,600]{1,0:T(8,128)S(1)} collective-permute-done((f32[32,600]{1,0:T(8,128)S(1)}, f32[32,600]{1,0:T(8,128)S(1)}, u32[]{:S(2)}, u32[]{:S(2)}) %collective-permute-start.2) | collective-permute-done | bytes 76832 | tf_op jit(solution)/shard_map/ppermute | solution.py:146
  13.0 0.0 collective-permute-done.3
  13.1 2.8 %collective-permute-start.4 = (f32[16,600]{1,0:T(8,128)S(1)}, f32[16,600]{1,0:T(8,128)S(1)}, u32[]{:S(2)}, u32[]{:S(2)}) collective-permute-start(f32[16,600]{1,0:T(8,128)S(1)} %split.9), channel_id=1, source_target_pairs={{0,8},{1,9},{2,10},{3,11},{4,12},{5,13},{6,14},{7,15},{8,0},{9,1},... | collective-permute-start | bytes 115208 | tf_op jit(solution)/shard_map/ppermute | solution.py:146
  15.9 2.1 %collective-permute-done.4 = f32[16,600]{1,0:T(8,128)S(1)} collective-permute-done((f32[16,600]{1,0:T(8,128)S(1)}, f32[16,600]{1,0:T(8,128)S(1)}, u32[]{:S(2)}, u32[]{:S(2)}) %collective-permute-start.4) | collective-permute-done | bytes 38432 | tf_op jit(solution)/shard_map/ppermute | solution.py:146
  18.1 0.6 %slice_add_fusion = f32[16,600]{1,0:T(8,128)} fusion(f32[16,600]{1,0:T(8,128)S(1)} %collective-permute-done.4, f32[32,600]{1,0:T(8,128)S(1)} %add_add_fusion), kind=kLoop, calls=%fused_computation.1 | loop fusion | flops 9600 | bytes 115200 | tf_op jit(solution)/shard_map/add | solution.py:146
  (2 shorter events, 0.0 us)
Async XLA Ops:
  2.5 1.8 %collective-permute-start = (f32[608,128]{1,0:T(8,128)S(1)}, f32[608,128]{1,0:T(8,128)S(1)}, u32[]{:S(2)}, u32[]{:S(2)}) collective-permute-start(f32[608,128]{1,0:T(8,128)S(1)} %get-tuple-element.12), channel_id=1, source_target_pairs={{0,1},{1,0},{2,3},{3,2},{4,5},{5,4},{6,7},{7,6},{8,9},{9,8},{10,11... | collective-permute-start | bytes 933896 | tf_op jit(solution)/shard_map/ppermute | solution.py:131
  4.4 7.0 %collective-permute-start.1 = (f32[32,600]{1,0:T(8,128)S(1)}, f32[32,600]{1,0:T(8,128)S(1)}, u32[]{:S(2)}, u32[]{:S(2)}) collective-permute-start(f32[32,600]{1,0:T(8,128)S(1)} %get-tuple-element.14), channel_id=1, source_target_pairs={{0,4},{1,5},{2,6},{3,7},{4,2},{5,3},{6,0},{7,1},{8,12},{9,13},{10,... | collective-permute-start | bytes 230408 | tf_op jit(solution)/shard_map/ppermute | solution.py:146
  7.4 5.6 %collective-permute-start.2 = (f32[32,600]{1,0:T(8,128)S(1)}, f32[32,600]{1,0:T(8,128)S(1)}, u32[]{:S(2)}, u32[]{:S(2)}) collective-permute-start(f32[32,600]{1,0:T(8,128)S(1)} %get-tuple-element.15), channel_id=1, source_target_pairs={{0,6},{1,7},{2,4},{3,5},{4,0},{5,1},{6,2},{7,3},{8,14},{9,15},{10,... | collective-permute-start | bytes 230408 | tf_op jit(solution)/shard_map/ppermute | solution.py:146
  8.4 4.6 %collective-permute-start.3 = (f32[32,600]{1,0:T(8,128)S(1)}, f32[32,600]{1,0:T(8,128)S(1)}, u32[]{:S(2)}, u32[]{:S(2)}) collective-permute-start(f32[32,600]{1,0:T(8,128)S(1)} %get-tuple-element.16), channel_id=1, source_target_pairs={{0,2},{1,3},{2,0},{3,1},{4,6},{5,7},{6,4},{7,5},{8,10},{9,11},{10,... | collective-permute-start | bytes 230408 | tf_op jit(solution)/shard_map/ppermute | solution.py:146
  13.1 5.0 %collective-permute-start.4 = (f32[16,600]{1,0:T(8,128)S(1)}, f32[16,600]{1,0:T(8,128)S(1)}, u32[]{:S(2)}, u32[]{:S(2)}) collective-permute-start(f32[16,600]{1,0:T(8,128)S(1)} %split.9), channel_id=1, source_target_pairs={{0,8},{1,9},{2,10},{3,11},{4,12},{5,13},{6,14},{7,15},{8,0},{9,1},... | collective-permute-start | bytes 115208 | tf_op jit(solution)/shard_map/ppermute | solution.py:146

commit v6 on v5

--- a/solution.py
+++ b/solution.py
@@ -12,19 +12,28 @@
 LANES = 128
 
 
-def phases(chips):
+def split_bits(chips):
     bits = chips.bit_length() - 1
-    fours = [(2 << b, [(0, 0), (2 << b, 3 << b), (3 << b, 2 << b), (1 << b, 1 << b)]) for b in range(0, bits - 1, 2)]
-    last = 1 << bits - 1
-    return fours + [(last, [(0, 0), (last, last)])] * (bits % 2)
+    return list(range(0, bits - 1, 2)), bits % 2
+
+
+def offsets(chips, b, chip):
+    parity = ((chip >> b) ^ (chip >> (b + 1))) & 1
+    near = (2 - parity, 1 + parity, 3)
+    far = (3, 2, 1)
+    is_far = (chip >> (chips.bit_length() - 2)) & 1 if split_bits(chips)[1] else 0
+    return [0] + [(n + is_far * (f - n)) << b for n, f in zip(near, far)]
 
 
 def owner_of(chips, chip, slot):
+    fours, pair = split_bits(chips)
     result = chip
-    for mask, offsets in reversed(phases(chips)):
-        slot, digit = divmod(slot, len(offsets))
-        clear, marked = offsets[digit]
-        result = jnp.bitwise_xor(result, jnp.where(jnp.bitwise_and(chip, mask) == 0, clear, marked))
+    if pair:
+        slot, digit = divmod(slot, 2)
+        result = result ^ (digit * (chips // 2))
+    for b in reversed(fours):
+        slot, digit = divmod(slot, 4)
+        result = result ^ offsets(chips, b, chip)[digit]
     return result
 
 
@@ -129,21 +138,35 @@
         name="dots",
     )(*(pltpu.with_memory_space_constraint(x, pltpu.HBM) for x in (train_grads, query_grads)))
     got = lax.ppermute(send, "docs", [(i, i ^ 1) for i in range(devices)])
-    exchanges = phases(chips)
-    count = len(exchanges[0][1])
+    fours, pair = split_bits(chips)
+    count = 4 if fours else 2
     parts = pl.pallas_call(
         functools.partial(scale_kernel, factor, queries),
         out_shape=[jax.ShapeDtypeStruct((half // count, queries), jnp.float32)] * count,
         compiler_params=pltpu.CompilerParams(vmem_limit_bytes=40 * 2**20),
         name="scale",
     )(keep, got)
-    for i, (mask, offsets) in enumerate(exchanges):
-        if i > 0:
-            parts = jnp.split(terms, len(offsets))
-        terms = parts[0]
-        for part, (clear, marked) in zip(parts[1:], offsets[1:]):
-            pairs = [(d, d ^ 2 * (marked if d // 2 & mask else clear)) for d in range(devices)]
-            terms = terms + lax.ppermute(part, "docs", pairs)
+
+    def move(part, b, i):
+        pairs = [(d, d ^ 2 * offsets(chips, b, d // 2)[i]) for d in range(devices)]
+        return lax.ppermute(part, "docs", pairs)
+
+    def cross(part):
+        return lax.ppermute(part, "docs", [(d, d ^ chips) for d in range(devices)])
+
+    for b in fours:
+        if b > 0:
+            parts = jnp.split(terms, 4)
+        if pair and b == fours[-1]:
+            size = parts[0].shape[0] // 2
+            first, second = move(parts[1], b, 1), move(parts[2], b, 2)
+            third_far = move(parts[3][size:], b, 3)
+            third_near = move(parts[3][:size], b, 3)
+            far = parts[0][size:] + first[size:] + second[size:] + third_far
+            return parts[0][:size] + first[:size] + second[:size] + third_near + cross(far)
+        terms = parts[0] + move(parts[1], b, 1) + move(parts[2], b, 2) + move(parts[3], b, 3)
+    if pair:
+        terms = parts[0] + cross(parts[1])
     return terms
 
 

time: 18.8 us -> 18.5 us (0.984)
  waiting for transfers between devices: 6.13 us -> 5.21 us
  starting transfers between devices: 9.2 us -> 9.84 us
    ppermute x4 -> x5, waiting for transfers between devices: 4.9 us -> 3.98 us  [the longest x1 2.05 us: cross(): return lax.ppermute(part, 'docs', [(d, d ^ chips) for d in range(devices)])]
    ppermute x4 -> x5, starting transfers between devices: 8.68 us -> 9.32 us  [the longest x4 6.08 us: move(): return lax.ppermute(part, 'docs', pairs)]
  transfers between devices with their start and end apart: 5 -> 6, of which waited for: 4 -> 3; matrix products, arithmetic and copies ran while one was open for 0% -> 0% of each run, Pallas kernels for 0% -> 0%
where the time goes in v6:
time: 18.5 us; the launch traced here: 18.4 us
  starting transfers between devices  9.84 us (53%)
  waiting for transfers between devices  5.21 us (28%)
  Pallas kernels  2.66 us (14%)
  other arithmetic  0.64 us (3%)
    ppermute x4, starting transfers between devices, move(): return lax.ppermute(part, 'docs', pairs)  6.08 us
    ppermute x1, starting transfers between devices, cross(): return lax.ppermute(part, 'docs', [(d, d ^ chips) for d in range(devices)])  3.24 us
    pallas_call x1, Pallas kernels, local(): pl.pallas_call(functools.partial(dots_kernel, chips, cuts), out_shape=[pa...  2.49 us
    ppermute x1, waiting for transfers between devices, cross(): return lax.ppermute(part, 'docs', [(d, d ^ chips) for d in range(devices)])  2.05 us
    ppermute x4, waiting for transfers between devices, move(): return lax.ppermute(part, 'docs', pairs)  1.93 us
    ppermute x1, waiting for transfers between devices, local(): got = lax.ppermute(send, 'docs', [(i, i ^ 1) for i in range(devices)])  1.23 us
    add x1, other arithmetic, local(): parts[0][:size] + first[:size] + second[:size] + third_near + cross(far)  0.63 us
    ppermute x1, starting transfers between devices, local(): got = lax.ppermute(send, 'docs', [(i, i ^ 1) for i in range(devices)])  0.52 us
  transfers between devices with their start and end apart: 6, of which 3 were waited for; matrix products, arithmetic and copies ran while one was open for 0% of the time, Pallas kernels for 0%

profile of v6, /device:TPU:0, one launch (start us, length us, event | category | flops | bytes accessed | tf_op | source)
XLA Modules:
  0.0 18.4 jit_solution(18201075654781142580)
XLA Ops:
  0.0 2.5 %dots.1 = (f32[608,128]{1,0:T(8,128)S(1)}, f32[608,128]{1,0:T(8,128)S(1)}) custom-call(bf16[256,2048]{1,0:T(8,128)(2,1)} %train.1, bf16[600,2048]{1,0:T(8,128)(2,1)} %query.1), custom_call_target="tpu_custom_call" | custom-call | tf_op jit(solution)/shard_map/dots/pallas_call | solution.py:125
  2.5 0.5 %collective-permute-start = (f32[608,128]{1,0:T(8,128)S(1)}, f32[608,128]{1,0:T(8,128)S(1)}, u32[]{:S(2)}, u32[]{:S(2)}) collective-permute-start(f32[608,128]{1,0:T(8,128)S(1)} %get-tuple-element.12), channel_id=1, source_target_pairs={{0,1},{1,0},{2,3},{3,2},{4,5},{5,4},{6,7},{7,6},{8,9},{9,8},{10,11... | collective-permute-start | bytes 933896 | tf_op jit(solution)/shard_map/ppermute | solution.py:140
  3.0 1.2 %collective-permute-done.got = f32[608,128]{1,0:T(8,128)S(1)} collective-permute-done((f32[608,128]{1,0:T(8,128)S(1)}, f32[608,128]{1,0:T(8,128)S(1)}, u32[]{:S(2)}, u32[]{:S(2)}) %collective-permute-start) | collective-permute-done | bytes 311328 | tf_op jit(solution)/shard_map/ppermute | solution.py:140
  4.2 0.2 scale.1
  4.4 3.0 %collective-permute-start.1 = (f32[32,600]{1,0:T(8,128)S(1)}, f32[32,600]{1,0:T(8,128)S(1)}, u32[]{:S(2)}, u32[]{:S(2)}) collective-permute-start(f32[32,600]{1,0:T(8,128)S(1)} %get-tuple-element.14), channel_id=1, source_target_pairs={{0,4},{1,5},{2,0},{3,1},{4,6},{5,7},{6,2},{7,3},{8,14},{9,15},{10,... | collective-permute-start | bytes 230408 | tf_op jit(solution)/shard_map/ppermute | solution.py:152
  7.5 0.0 collective-permute-start.2
  7.5 2.9 %collective-permute-start.4 = (f32[16,600]{1,0:T(8,128)S(1)}, f32[16,600]{1,0:T(8,128)S(1)}, u32[]{:S(2)}, u32[]{:S(2)}) collective-permute-start(f32[16,600]{1,0:T(8,128)S(1)} %get-tuple-element.18), channel_id=1, source_target_pairs={{0,6},{1,7},{2,4},{3,5},{4,2},{5,3},{6,0},{7,1},{8,10},{9,11},{10,... | collective-permute-start | bytes 115208 | tf_op jit(solution)/shard_map/ppermute | solution.py:152
  10.4 0.1 collective-permute-start.3
  10.5 1.9 %collective-permute-done.4 = f32[16,600]{1,0:T(8,128)S(1)} collective-permute-done((f32[16,600]{1,0:T(8,128)S(1)}, f32[16,600]{1,0:T(8,128)S(1)}, u32[]{:S(2)}, u32[]{:S(2)}) %collective-permute-start.4) | collective-permute-done | bytes 38432 | tf_op jit(solution)/shard_map/ppermute | solution.py:152
  12.4 0.0 collective-permute-done.1
  12.4 0.0 collective-permute-done.2
  12.5 3.2 %collective-permute-start.5 = (f32[16,600]{1,0:T(8,128)S(1)}, f32[16,600]{1,0:T(8,128)S(1)}, u32[]{:S(2)}, u32[]{:S(2)}) collective-permute-start(f32[16,600]{1,0:T(8,128)S(1)} %fusion), channel_id=1, source_target_pairs={{0,8},{1,9},{2,10},{3,11},{4,12},{5,13},{6,14},{7,15},{8,0},{9,1},... | collective-permute-start | bytes 115208 | tf_op jit(solution)/shard_map/ppermute | solution.py:155
  15.7 0.0 collective-permute-done.3
  15.7 2.0 %collective-permute-done.5 = f32[16,600]{1,0:T(8,128)S(1)} collective-permute-done((f32[16,600]{1,0:T(8,128)S(1)}, f32[16,600]{1,0:T(8,128)S(1)}, u32[]{:S(2)}, u32[]{:S(2)}) %collective-permute-start.5) | collective-permute-done | bytes 38432 | tf_op jit(solution)/shard_map/ppermute | solution.py:155
  17.8 0.6 %fusion.2 = f32[16,600]{1,0:T(8,128)} fusion(f32[16,600]{1,0:T(8,128)S(1)} %collective-permute-done.5, f32[16,600]{1,0:T(8,128)S(1)} %collective-permute-done.3, f32[32,600]{1,0:T(8,128)S(1)} %collective-permute-done.2, f32[32,600]{1,0:T(8,128)S(1)} %collective-permute-done.1, f32[32,600]{1,0:T(8,128)S(1)} %get-tuple-element.13), kind=kLoop, calls=%fused_computation.5 | loop fusion | flops 38400 | bytes 230400 | tf_op jit(solution)/shard_map/add | solution.py:166
  (2 shorter events, 0.0 us)
Async XLA Ops:
  2.5 1.8 %collective-permute-start = (f32[608,128]{1,0:T(8,128)S(1)}, f32[608,128]{1,0:T(8,128)S(1)}, u32[]{:S(2)}, u32[]{:S(2)}) collective-permute-start(f32[608,128]{1,0:T(8,128)S(1)} %get-tuple-element.12), channel_id=1, source_target_pairs={{0,1},{1,0},{2,3},{3,2},{4,5},{5,4},{6,7},{7,6},{8,9},{9,8},{10,11... | collective-permute-start | bytes 933896 | tf_op jit(solution)/shard_map/ppermute | solution.py:140
  4.4 8.0 %collective-permute-start.1 = (f32[32,600]{1,0:T(8,128)S(1)}, f32[32,600]{1,0:T(8,128)S(1)}, u32[]{:S(2)}, u32[]{:S(2)}) collective-permute-start(f32[32,600]{1,0:T(8,128)S(1)} %get-tuple-element.14), channel_id=1, source_target_pairs={{0,4},{1,5},{2,0},{3,1},{4,6},{5,7},{6,2},{7,3},{8,14},{9,15},{10,... | collective-permute-start | bytes 230408 | tf_op jit(solution)/shard_map/ppermute | solution.py:152
  7.5 5.0 %collective-permute-start.2 = (f32[32,600]{1,0:T(8,128)S(1)}, f32[32,600]{1,0:T(8,128)S(1)}, u32[]{:S(2)}, u32[]{:S(2)}) collective-permute-start(f32[32,600]{1,0:T(8,128)S(1)} %get-tuple-element.15), channel_id=1, source_target_pairs={{0,2},{1,3},{2,6},{3,7},{4,0},{5,1},{6,4},{7,5},{8,12},{9,13},{10,... | collective-permute-start | bytes 230408 | tf_op jit(solution)/shard_map/ppermute | solution.py:152
  7.5 5.0 %collective-permute-start.4 = (f32[16,600]{1,0:T(8,128)S(1)}, f32[16,600]{1,0:T(8,128)S(1)}, u32[]{:S(2)}, u32[]{:S(2)}) collective-permute-start(f32[16,600]{1,0:T(8,128)S(1)} %get-tuple-element.18), channel_id=1, source_target_pairs={{0,6},{1,7},{2,4},{3,5},{4,2},{5,3},{6,0},{7,1},{8,10},{9,11},{10,... | collective-permute-start | bytes 115208 | tf_op jit(solution)/shard_map/ppermute | solution.py:152
  10.4 5.3 %collective-permute-start.3 = (f32[16,600]{1,0:T(8,128)S(1)}, f32[16,600]{1,0:T(8,128)S(1)}, u32[]{:S(2)}, u32[]{:S(2)}) collective-permute-start(f32[16,600]{1,0:T(8,128)S(1)} %get-tuple-element.17), channel_id=1, source_target_pairs={{0,6},{1,7},{2,4},{3,5},{4,2},{5,3},{6,0},{7,1},{8,10},{9,11},{10,... | collective-permute-start | bytes 115208 | tf_op jit(solution)/shard_map/ppermute | solution.py:152
  12.5 5.3 %collective-permute-start.5 = (f32[16,600]{1,0:T(8,128)S(1)}, f32[16,600]{1,0:T(8,128)S(1)}, u32[]{:S(2)}, u32[]{:S(2)}) collective-permute-start(f32[16,600]{1,0:T(8,128)S(1)} %fusion), channel_id=1, source_target_pairs={{0,8},{1,9},{2,10},{3,11},{4,12},{5,13},{6,14},{7,15},{8,0},{9,1},... | collective-permute-start | bytes 115208 | tf_op jit(solution)/shard_map/ppermute | solution.py:155

commit v7 on v6

--- a/solution.py
+++ b/solution.py
@@ -17,12 +17,9 @@
     return list(range(0, bits - 1, 2)), bits % 2
 
 
-def offsets(chips, b, chip):
+def offsets(b, chip):
     parity = ((chip >> b) ^ (chip >> (b + 1))) & 1
-    near = (2 - parity, 1 + parity, 3)
-    far = (3, 2, 1)
-    is_far = (chip >> (chips.bit_length() - 2)) & 1 if split_bits(chips)[1] else 0
-    return [0] + [(n + is_far * (f - n)) << b for n, f in zip(near, far)]
+    return [0] + [offset << b for offset in (2 - parity, 1 + parity, 3)]
 
 
 def owner_of(chips, chip, slot):
@@ -33,7 +30,7 @@
         result = result ^ (digit * (chips // 2))
     for b in reversed(fours):
         slot, digit = divmod(slot, 4)
-        result = result ^ offsets(chips, b, chip)[digit]
+        result = result ^ offsets(b, chip)[digit]
     return result
 
 
@@ -148,7 +145,7 @@
     )(keep, got)
 
     def move(part, b, i):
-        pairs = [(d, d ^ 2 * offsets(chips, b, d // 2)[i]) for d in range(devices)]
+        pairs = [(d, d ^ 2 * offsets(b, d // 2)[i]) for d in range(devices)]
         return lax.ppermute(part, "docs", pairs)
 
     def cross(part):

time: 18.5 us -> 18.2 us (0.984)
  starting transfers between devices: 9.84 us -> 9.6 us
    ppermute x1, starting transfers between devices: 3.24 us -> 3.03 us  [cross(): return lax.ppermute(part, 'docs', [(d, d ^ chips) for d in range(devices)])]
where the time goes in v7:
time: 18.2 us; the launch traced here: 18.1 us
  starting transfers between devices  9.6 us (53%)
  waiting for transfers between devices  5.14 us (28%)
  Pallas kernels  2.66 us (15%)
  other arithmetic  0.64 us (4%)
    ppermute x4, starting transfers between devices, move(): return lax.ppermute(part, 'docs', pairs)  6.05 us
    ppermute x1, starting transfers between devices, cross(): return lax.ppermute(part, 'docs', [(d, d ^ chips) for d in range(devices)])  3.03 us
    pallas_call x1, Pallas kernels, local(): pl.pallas_call(functools.partial(dots_kernel, chips, cuts), out_shape=[pa...  2.49 us
    ppermute x1, waiting for transfers between devices, cross(): return lax.ppermute(part, 'docs', [(d, d ^ chips) for d in range(devices)])  1.98 us
    ppermute x4, waiting for transfers between devices, move(): return lax.ppermute(part, 'docs', pairs)  1.93 us
    ppermute x1, waiting for transfers between devices, local(): got = lax.ppermute(send, 'docs', [(i, i ^ 1) for i in range(devices)])  1.23 us
    add x1, other arithmetic, local(): parts[0][:size] + first[:size] + second[:size] + third_near + cross(far)  0.63 us
    ppermute x1, starting transfers between devices, local(): got = lax.ppermute(send, 'docs', [(i, i ^ 1) for i in range(devices)])  0.52 us
  transfers between devices with their start and end apart: 6, of which 3 were waited for; matrix products, arithmetic and copies ran while one was open for 0% of the time, Pallas kernels for 0%

profile of v7, /device:TPU:0, one launch (start us, length us, event | category | flops | bytes accessed | tf_op | source)
XLA Modules:
  0.0 18.1 jit_solution(8816744080584303375)
XLA Ops:
  0.0 2.5 %dots.1 = (f32[608,128]{1,0:T(8,128)S(1)}, f32[608,128]{1,0:T(8,128)S(1)}) custom-call(bf16[256,2048]{1,0:T(8,128)(2,1)} %train.1, bf16[600,2048]{1,0:T(8,128)(2,1)} %query.1), custom_call_target="tpu_custom_call" | custom-call | tf_op jit(solution)/shard_map/dots/pallas_call | solution.py:122
  2.5 0.5 %collective-permute-start = (f32[608,128]{1,0:T(8,128)S(1)}, f32[608,128]{1,0:T(8,128)S(1)}, u32[]{:S(2)}, u32[]{:S(2)}) collective-permute-start(f32[608,128]{1,0:T(8,128)S(1)} %get-tuple-element.12), channel_id=1, source_target_pairs={{0,1},{1,0},{2,3},{3,2},{4,5},{5,4},{6,7},{7,6},{8,9},{9,8},{10,11... | collective-permute-start | bytes 933896 | tf_op jit(solution)/shard_map/ppermute | solution.py:137
  3.0 1.2 %collective-permute-done.got = f32[608,128]{1,0:T(8,128)S(1)} collective-permute-done((f32[608,128]{1,0:T(8,128)S(1)}, f32[608,128]{1,0:T(8,128)S(1)}, u32[]{:S(2)}, u32[]{:S(2)}) %collective-permute-start) | collective-permute-done | bytes 311328 | tf_op jit(solution)/shard_map/ppermute | solution.py:137
  4.2 0.2 scale.1
  4.4 3.0 %collective-permute-start.1 = (f32[32,600]{1,0:T(8,128)S(1)}, f32[32,600]{1,0:T(8,128)S(1)}, u32[]{:S(2)}, u32[]{:S(2)}) collective-permute-start(f32[32,600]{1,0:T(8,128)S(1)} %get-tuple-element.14), channel_id=1, source_target_pairs={{0,4},{1,5},{2,0},{3,1},{4,6},{5,7},{6,2},{7,3},{8,12},{9,13},{10,... | collective-permute-start | bytes 230408 | tf_op jit(solution)/shard_map/ppermute | solution.py:149
  7.4 0.0 collective-permute-start.2
  7.4 3.0 %collective-permute-start.4 = (f32[16,600]{1,0:T(8,128)S(1)}, f32[16,600]{1,0:T(8,128)S(1)}, u32[]{:S(2)}, u32[]{:S(2)}) collective-permute-start(f32[16,600]{1,0:T(8,128)S(1)} %get-tuple-element.18), channel_id=1, source_target_pairs={{0,6},{1,7},{2,4},{3,5},{4,2},{5,3},{6,0},{7,1},{8,14},{9,15},{10,... | collective-permute-start | bytes 115208 | tf_op jit(solution)/shard_map/ppermute | solution.py:149
  10.4 0.1 collective-permute-start.3
  10.5 1.9 %collective-permute-done.4 = f32[16,600]{1,0:T(8,128)S(1)} collective-permute-done((f32[16,600]{1,0:T(8,128)S(1)}, f32[16,600]{1,0:T(8,128)S(1)}, u32[]{:S(2)}, u32[]{:S(2)}) %collective-permute-start.4) | collective-permute-done | bytes 38432 | tf_op jit(solution)/shard_map/ppermute | solution.py:149
  12.4 0.0 collective-permute-done.1
  12.4 0.0 collective-permute-done.2
  12.4 3.0 %collective-permute-start.5 = (f32[16,600]{1,0:T(8,128)S(1)}, f32[16,600]{1,0:T(8,128)S(1)}, u32[]{:S(2)}, u32[]{:S(2)}) collective-permute-start(f32[16,600]{1,0:T(8,128)S(1)} %fusion), channel_id=1, source_target_pairs={{0,8},{1,9},{2,10},{3,11},{4,12},{5,13},{6,14},{7,15},{8,0},{9,1},... | collective-permute-start | bytes 115208 | tf_op jit(solution)/shard_map/ppermute | solution.py:152
  15.5 0.0 collective-permute-done.3
  15.5 2.0 %collective-permute-done.5 = f32[16,600]{1,0:T(8,128)S(1)} collective-permute-done((f32[16,600]{1,0:T(8,128)S(1)}, f32[16,600]{1,0:T(8,128)S(1)}, u32[]{:S(2)}, u32[]{:S(2)}) %collective-permute-start.5) | collective-permute-done | bytes 38432 | tf_op jit(solution)/shard_map/ppermute | solution.py:152
  17.4 0.6 %fusion.2 = f32[16,600]{1,0:T(8,128)} fusion(f32[16,600]{1,0:T(8,128)S(1)} %collective-permute-done.5, f32[16,600]{1,0:T(8,128)S(1)} %collective-permute-done.3, f32[32,600]{1,0:T(8,128)S(1)} %collective-permute-done.2, f32[32,600]{1,0:T(8,128)S(1)} %collective-permute-done.1, f32[32,600]{1,0:T(8,128)S(1)} %get-tuple-element.13), kind=kLoop, calls=%fused_computation.5 | loop fusion | flops 38400 | bytes 230400 | tf_op jit(solution)/shard_map/add | solution.py:163
  (2 shorter events, 0.0 us)
Async XLA Ops:
  2.5 1.8 %collective-permute-start = (f32[608,128]{1,0:T(8,128)S(1)}, f32[608,128]{1,0:T(8,128)S(1)}, u32[]{:S(2)}, u32[]{:S(2)}) collective-permute-start(f32[608,128]{1,0:T(8,128)S(1)} %get-tuple-element.12), channel_id=1, source_target_pairs={{0,1},{1,0},{2,3},{3,2},{4,5},{5,4},{6,7},{7,6},{8,9},{9,8},{10,11... | collective-permute-start | bytes 933896 | tf_op jit(solution)/shard_map/ppermute | solution.py:137
  4.4 8.0 %collective-permute-start.1 = (f32[32,600]{1,0:T(8,128)S(1)}, f32[32,600]{1,0:T(8,128)S(1)}, u32[]{:S(2)}, u32[]{:S(2)}) collective-permute-start(f32[32,600]{1,0:T(8,128)S(1)} %get-tuple-element.14), channel_id=1, source_target_pairs={{0,4},{1,5},{2,0},{3,1},{4,6},{5,7},{6,2},{7,3},{8,12},{9,13},{10,... | collective-permute-start | bytes 230408 | tf_op jit(solution)/shard_map/ppermute | solution.py:149
  7.4 5.0 %collective-permute-start.2 = (f32[32,600]{1,0:T(8,128)S(1)}, f32[32,600]{1,0:T(8,128)S(1)}, u32[]{:S(2)}, u32[]{:S(2)}) collective-permute-start(f32[32,600]{1,0:T(8,128)S(1)} %get-tuple-element.15), channel_id=1, source_target_pairs={{0,2},{1,3},{2,6},{3,7},{4,0},{5,1},{6,4},{7,5},{8,10},{9,11},{10,... | collective-permute-start | bytes 230408 | tf_op jit(solution)/shard_map/ppermute | solution.py:149
  7.4 5.0 %collective-permute-start.4 = (f32[16,600]{1,0:T(8,128)S(1)}, f32[16,600]{1,0:T(8,128)S(1)}, u32[]{:S(2)}, u32[]{:S(2)}) collective-permute-start(f32[16,600]{1,0:T(8,128)S(1)} %get-tuple-element.18), channel_id=1, source_target_pairs={{0,6},{1,7},{2,4},{3,5},{4,2},{5,3},{6,0},{7,1},{8,14},{9,15},{10,... | collective-permute-start | bytes 115208 | tf_op jit(solution)/shard_map/ppermute | solution.py:149
  10.4 5.1 %collective-permute-start.3 = (f32[16,600]{1,0:T(8,128)S(1)}, f32[16,600]{1,0:T(8,128)S(1)}, u32[]{:S(2)}, u32[]{:S(2)}) collective-permute-start(f32[16,600]{1,0:T(8,128)S(1)} %get-tuple-element.17), channel_id=1, source_target_pairs={{0,6},{1,7},{2,4},{3,5},{4,2},{5,3},{6,0},{7,1},{8,14},{9,15},{10,... | collective-permute-start | bytes 115208 | tf_op jit(solution)/shard_map/ppermute | solution.py:149
  12.4 5.0 %collective-permute-start.5 = (f32[16,600]{1,0:T(8,128)S(1)}, f32[16,600]{1,0:T(8,128)S(1)}, u32[]{:S(2)}, u32[]{:S(2)}) collective-permute-start(f32[16,600]{1,0:T(8,128)S(1)} %fusion), channel_id=1, source_target_pairs={{0,8},{1,9},{2,10},{3,11},{4,12},{5,13},{6,14},{7,15},{8,0},{9,1},... | collective-permute-start | bytes 115208 | tf_op jit(solution)/shard_map/ppermute | solution.py:152

commit v8 on v7

--- a/solution.py
+++ b/solution.py
@@ -104,9 +104,10 @@
         parts.append(keep[row : row + 1, :width] + got[row : row + 1, :width])
     query = lax.rsqrt(jnp.concatenate(parts, axis=1) + EPS)
     total = ((keep[:queries, :] + got[:queries, :]) * doc).T * query
-    size = terms[0].shape[0]
-    for i, part in enumerate(terms):
-        part[...] = total[i * size : (i + 1) * size, :]
+    low = 0
+    for part in terms:
+        part[...] = total[low : low + part.shape[0], :]
+        low += part.shape[0]
 
 
 def local(train_grads, query_grads):
@@ -137,9 +138,12 @@
     got = lax.ppermute(send, "docs", [(i, i ^ 1) for i in range(devices)])
     fours, pair = split_bits(chips)
     count = 4 if fours else 2
+    heights = [half // count] * count
+    if pair and len(fours) == 1:
+        heights = heights[:-1] + [half // count // 2] * 2
     parts = pl.pallas_call(
         functools.partial(scale_kernel, factor, queries),
-        out_shape=[jax.ShapeDtypeStruct((half // count, queries), jnp.float32)] * count,
+        out_shape=[jax.ShapeDtypeStruct((r, queries), jnp.float32) for r in heights],
         compiler_params=pltpu.CompilerParams(vmem_limit_bytes=40 * 2**20),
         name="scale",
     )(keep, got)
@@ -156,9 +160,10 @@
             parts = jnp.split(terms, 4)
         if pair and b == fours[-1]:
             size = parts[0].shape[0] // 2
+            last = parts[3:] if len(parts) == 5 else [parts[3][:size], parts[3][size:]]
             first, second = move(parts[1], b, 1), move(parts[2], b, 2)
-            third_far = move(parts[3][size:], b, 3)
-            third_near = move(parts[3][:size], b, 3)
+            third_far = move(last[1], b, 3)
+            third_near = move(last[0], b, 3)
             far = parts[0][size:] + first[size:] + second[size:] + third_far
             return parts[0][:size] + first[:size] + second[:size] + third_near + cross(far)
         terms = parts[0] + move(parts[1], b, 1) + move(parts[2], b, 2) + move(parts[3], b, 3)

time: 18.2 us -> 18.2 us (level)
  no operation moved by 1% of the time
where the time goes in v8:
time: 18.2 us; the launch traced here: 18.1 us
  starting transfers between devices  9.58 us (53%)
  waiting for transfers between devices  5.16 us (28%)
  Pallas kernels  2.66 us (15%)
  other arithmetic  0.64 us (4%)
    ppermute x4, starting transfers between devices, move(): return lax.ppermute(part, 'docs', pairs)  6.01 us
    ppermute x1, starting transfers between devices, cross(): return lax.ppermute(part, 'docs', [(d, d ^ chips) for d in range(devices)])  3.05 us
    pallas_call x1, Pallas kernels, local(): pl.pallas_call(functools.partial(dots_kernel, chips, cuts), out_shape=[pa...  2.49 us
    ppermute x1, waiting for transfers between devices, cross(): return lax.ppermute(part, 'docs', [(d, d ^ chips) for d in range(devices)])  1.98 us
    ppermute x4, waiting for transfers between devices, move(): return lax.ppermute(part, 'docs', pairs)  1.95 us
    ppermute x1, waiting for transfers between devices, local(): got = lax.ppermute(send, 'docs', [(i, i ^ 1) for i in range(devices)])  1.23 us
    add x1, other arithmetic, local(): parts[0][:size] + first[:size] + second[:size] + third_near + cross(far)  0.63 us
    ppermute x1, starting transfers between devices, local(): got = lax.ppermute(send, 'docs', [(i, i ^ 1) for i in range(devices)])  0.52 us
  transfers between devices with their start and end apart: 6, of which 3 were waited for; matrix products, arithmetic and copies ran while one was open for 0% of the time, Pallas kernels for 0%

profile of v8, /device:TPU:0, one launch (start us, length us, event | category | flops | bytes accessed | tf_op | source)
XLA Modules:
  0.0 18.1 jit_solution(9983860793695188600)
XLA Ops:
  0.0 2.5 %dots.1 = (f32[608,128]{1,0:T(8,128)S(1)}, f32[608,128]{1,0:T(8,128)S(1)}) custom-call(bf16[256,2048]{1,0:T(8,128)(2,1)} %train.1, bf16[600,2048]{1,0:T(8,128)(2,1)} %query.1), custom_call_target="tpu_custom_call" | custom-call | tf_op jit(solution)/shard_map/dots/pallas_call | solution.py:123
  2.5 0.5 %collective-permute-start = (f32[608,128]{1,0:T(8,128)S(1)}, f32[608,128]{1,0:T(8,128)S(1)}, u32[]{:S(2)}, u32[]{:S(2)}) collective-permute-start(f32[608,128]{1,0:T(8,128)S(1)} %get-tuple-element.13), channel_id=1, source_target_pairs={{0,1},{1,0},{2,3},{3,2},{4,5},{5,4},{6,7},{7,6},{8,9},{9,8},{10,11... | collective-permute-start | bytes 933896 | tf_op jit(solution)/shard_map/ppermute | solution.py:138
  3.0 1.2 %collective-permute-done.got = f32[608,128]{1,0:T(8,128)S(1)} collective-permute-done((f32[608,128]{1,0:T(8,128)S(1)}, f32[608,128]{1,0:T(8,128)S(1)}, u32[]{:S(2)}, u32[]{:S(2)}) %collective-permute-start) | collective-permute-done | bytes 311328 | tf_op jit(solution)/shard_map/ppermute | solution.py:138
  4.2 0.2 scale.1
  4.4 3.0 %collective-permute-start.1 = (f32[32,600]{1,0:T(8,128)S(1)}, f32[32,600]{1,0:T(8,128)S(1)}, u32[]{:S(2)}, u32[]{:S(2)}) collective-permute-start(f32[32,600]{1,0:T(8,128)S(1)} %get-tuple-element.15), channel_id=1, source_target_pairs={{0,4},{1,5},{2,0},{3,1},{4,6},{5,7},{6,2},{7,3},{8,12},{9,13},{10,... | collective-permute-start | bytes 230408 | tf_op jit(solution)/shard_map/ppermute | solution.py:153
  7.4 0.0 collective-permute-start.2
  7.4 3.0 %collective-permute-start.4 = (f32[16,600]{1,0:T(8,128)S(1)}, f32[16,600]{1,0:T(8,128)S(1)}, u32[]{:S(2)}, u32[]{:S(2)}) collective-permute-start(f32[16,600]{1,0:T(8,128)S(1)} %get-tuple-element.18), channel_id=1, source_target_pairs={{0,6},{1,7},{2,4},{3,5},{4,2},{5,3},{6,0},{7,1},{8,14},{9,15},{10,... | collective-permute-start | bytes 115208 | tf_op jit(solution)/shard_map/ppermute | solution.py:153
  10.4 0.0 collective-permute-start.3
  10.4 1.9 %collective-permute-done.4 = f32[16,600]{1,0:T(8,128)S(1)} collective-permute-done((f32[16,600]{1,0:T(8,128)S(1)}, f32[16,600]{1,0:T(8,128)S(1)}, u32[]{:S(2)}, u32[]{:S(2)}) %collective-permute-start.4) | collective-permute-done | bytes 38432 | tf_op jit(solution)/shard_map/ppermute | solution.py:153
  12.4 0.0 collective-permute-done.1
  12.4 0.0 collective-permute-done.2
  12.4 3.0 %collective-permute-start.5 = (f32[16,600]{1,0:T(8,128)S(1)}, f32[16,600]{1,0:T(8,128)S(1)}, u32[]{:S(2)}, u32[]{:S(2)}) collective-permute-start(f32[16,600]{1,0:T(8,128)S(1)} %fusion), channel_id=1, source_target_pairs={{0,8},{1,9},{2,10},{3,11},{4,12},{5,13},{6,14},{7,15},{8,0},{9,1},... | collective-permute-start | bytes 115208 | tf_op jit(solution)/shard_map/ppermute | solution.py:156
  15.5 0.0 collective-permute-done.3
  15.5 2.0 %collective-permute-done.5 = f32[16,600]{1,0:T(8,128)S(1)} collective-permute-done((f32[16,600]{1,0:T(8,128)S(1)}, f32[16,600]{1,0:T(8,128)S(1)}, u32[]{:S(2)}, u32[]{:S(2)}) %collective-permute-start.5) | collective-permute-done | bytes 38432 | tf_op jit(solution)/shard_map/ppermute | solution.py:156
  17.4 0.6 %fusion.2 = f32[16,600]{1,0:T(8,128)} fusion(f32[16,600]{1,0:T(8,128)S(1)} %collective-permute-done.5, f32[16,600]{1,0:T(8,128)S(1)} %collective-permute-done.3, f32[32,600]{1,0:T(8,128)S(1)} %collective-permute-done.2, f32[32,600]{1,0:T(8,128)S(1)} %collective-permute-done.1, f32[32,600]{1,0:T(8,128)S(1)} %get-tuple-element.14), kind=kLoop, calls=%fused_computation.5 | loop fusion | flops 38400 | bytes 230400 | tf_op jit(solution)/shard_map/add | solution.py:168
  (1 shorter events, 0.0 us)
Async XLA Ops:
  2.5 1.8 %collective-permute-start = (f32[608,128]{1,0:T(8,128)S(1)}, f32[608,128]{1,0:T(8,128)S(1)}, u32[]{:S(2)}, u32[]{:S(2)}) collective-permute-start(f32[608,128]{1,0:T(8,128)S(1)} %get-tuple-element.13), channel_id=1, source_target_pairs={{0,1},{1,0},{2,3},{3,2},{4,5},{5,4},{6,7},{7,6},{8,9},{9,8},{10,11... | collective-permute-start | bytes 933896 | tf_op jit(solution)/shard_map/ppermute | solution.py:138
  4.4 8.0 %collective-permute-start.1 = (f32[32,600]{1,0:T(8,128)S(1)}, f32[32,600]{1,0:T(8,128)S(1)}, u32[]{:S(2)}, u32[]{:S(2)}) collective-permute-start(f32[32,600]{1,0:T(8,128)S(1)} %get-tuple-element.15), channel_id=1, source_target_pairs={{0,4},{1,5},{2,0},{3,1},{4,6},{5,7},{6,2},{7,3},{8,12},{9,13},{10,... | collective-permute-start | bytes 230408 | tf_op jit(solution)/shard_map/ppermute | solution.py:153
  7.4 5.0 %collective-permute-start.2 = (f32[32,600]{1,0:T(8,128)S(1)}, f32[32,600]{1,0:T(8,128)S(1)}, u32[]{:S(2)}, u32[]{:S(2)}) collective-permute-start(f32[32,600]{1,0:T(8,128)S(1)} %get-tuple-element.16), channel_id=1, source_target_pairs={{0,2},{1,3},{2,6},{3,7},{4,0},{5,1},{6,4},{7,5},{8,10},{9,11},{10,... | collective-permute-start | bytes 230408 | tf_op jit(solution)/shard_map/ppermute | solution.py:153
  7.4 5.0 %collective-permute-start.4 = (f32[16,600]{1,0:T(8,128)S(1)}, f32[16,600]{1,0:T(8,128)S(1)}, u32[]{:S(2)}, u32[]{:S(2)}) collective-permute-start(f32[16,600]{1,0:T(8,128)S(1)} %get-tuple-element.18), channel_id=1, source_target_pairs={{0,6},{1,7},{2,4},{3,5},{4,2},{5,3},{6,0},{7,1},{8,14},{9,15},{10,... | collective-permute-start | bytes 115208 | tf_op jit(solution)/shard_map/ppermute | solution.py:153
  10.4 5.1 %collective-permute-start.3 = (f32[16,600]{1,0:T(8,128)S(1)}, f32[16,600]{1,0:T(8,128)S(1)}, u32[]{:S(2)}, u32[]{:S(2)}) collective-permute-start(f32[16,600]{1,0:T(8,128)S(1)} %get-tuple-element.17), channel_id=1, source_target_pairs={{0,6},{1,7},{2,4},{3,5},{4,2},{5,3},{6,0},{7,1},{8,14},{9,15},{10,... | collective-permute-start | bytes 115208 | tf_op jit(solution)/shard_map/ppermute | solution.py:153
  12.4 5.0 %collective-permute-start.5 = (f32[16,600]{1,0:T(8,128)S(1)}, f32[16,600]{1,0:T(8,128)S(1)}, u32[]{:S(2)}, u32[]{:S(2)}) collective-permute-start(f32[16,600]{1,0:T(8,128)S(1)} %fusion), channel_id=1, source_target_pairs={{0,8},{1,9},{2,10},{3,11},{4,12},{5,13},{6,14},{7,15},{8,0},{9,1},... | collective-permute-start | bytes 115208 | tf_op jit(solution)/shard_map/ppermute | solution.py:156
